TPU v7x, 256 devices: a whole 4x4x8 slice. The times are simulated.
256 devices in a mesh: row: 16 (over y, x_hi, core), col: 16 (over z, x_lo).
Axes of the slice: x: 4 (x_hi: 2, x_lo: 2; x = x_hi * 2 + x_lo), y: 4, z: 8, core: 2. Of those that a mesh axis runs over, the one named last changes fastest.
Arguments:
- queries: bfloat16 [8192, 2048], P('row'), may hold values from -6 to 6
- keys: bfloat16 [4096, 2048], P('col'), may hold values from -6 to 6
- values: bfloat16 [4096, 2048], P('col'), may hold values from -6 to 6
- out_grad: bfloat16 [8192, 2048], P('row'), may hold values from -6 to 6
- tau: float32 [16, 8192], P(None, 'row'), may hold values from 2 to 3.5
- alpha: float32 [16], replicated, may hold values from 1.25 to 1.75
- query_blocks: int32 [64], P('row'), may hold values from 0 to 31
- key_blocks: int32 [32], P('col'), may hold values from 0 to 31, each once
Outputs:
- query_grad: bfloat16 [2048, 8192], P('col', 'row')
- key_grad: bfloat16 [2048, 4096], P('row', 'col')
- value_grad: bfloat16 [2048, 4096], P('row', 'col')
All inputs are finite; a program needn't handle non-finite values.
Results may differ from a plain program's by a relative error of at most 0.007.
Values may be sent and summed in bfloat16 or wider, within the bound.
A program may use at most 128 MiB of HBM per device.

v0:
```python
import math

import jax
import jax.numpy as jnp
from jax import lax
from jax.sharding import PartitionSpec as P

H = 16
DH = 128
BLK = 128


def block_positions(blocks, block_size):
    within = jnp.arange(block_size, dtype=jnp.int32)
    return (blocks[:, None] * block_size + within[None, :]).reshape(-1)


def local(queries, keys, values, out_grad, tau, alpha, query_blocks, key_blocks):
    factor = 1.0 / math.sqrt(DH)
    query_count = queries.shape[0]
    key_count = keys.shape[0]
    allowed = (
        block_positions(key_blocks, BLK)[None, :] <= block_positions(query_blocks, BLK)[:, None]
    )
    head_ids = jnp.arange(H, dtype=jnp.int32)

    def head_parts(head):
        query_head = lax.dynamic_slice_in_dim(queries, head * DH, DH, 1)
        key_head = lax.dynamic_slice_in_dim(keys, head * DH, DH, 1)
        value_head = lax.dynamic_slice_in_dim(values, head * DH, DH, 1)
        grad_head = lax.dynamic_slice_in_dim(out_grad, head * DH, DH, 1)
        excess = alpha[head] - 1.0
        scores = (
            jnp.einsum("qd,kd->qk", query_head, key_head, preferred_element_type=jnp.float32)
            * factor
        )
        support = jnp.where(allowed, jnp.maximum(excess * (scores - tau[head][:, None]), 0.0), 0.0)
        weights_h = support ** ((1.0 - excess) / excess)
        prob_grad_h = jnp.einsum(
            "qd,kd->qk", grad_head, value_head, preferred_element_type=jnp.float32
        )
        return (support, weights_h, prob_grad_h, excess)

    def first_pass(head):
        support, weights_h, prob_grad_h, excess = head_parts(head)
        probs_h = (support ** (1.0 / excess)).astype(jnp.bfloat16)
        return (probs_h, jnp.sum(weights_h * prob_grad_h, axis=1), jnp.sum(weights_h, axis=1))

    probabilities, totals, masses = lax.map(first_pass, head_ids)
    totals, masses = lax.psum((totals, masses), "col")
    row_shift = totals / jnp.maximum(masses, 1.0)
    row_share = queries.shape[1] // lax.axis_size("row")
    col_share = queries.shape[1] // lax.axis_size("col")

    def key_side(row_count, left, right):
        number = row_count // DH
        columns = right.reshape(query_count, number, DH)
        return jnp.einsum(
            "hqk,qhd->hdk", left, columns, preferred_element_type=jnp.float32
        ).reshape(row_count, key_count)

    def second_pass(head):
        support, weights_h, prob_grad_h, excess = head_parts(head)
        return (weights_h * (prob_grad_h - row_shift[head][:, None])).astype(jnp.bfloat16)

    score_grad = lax.map(second_pass, head_ids)
    number = lax.axis_size("col") * col_share // DH
    columns = keys.reshape(key_count, number, DH)
    query_grad = lax.psum_scatter(
        factor
        * jnp.einsum(
            "hqk,khd->hdq", score_grad, columns, preferred_element_type=jnp.float32
        ).reshape(lax.axis_size("col") * col_share, query_count),
        "col",
        scatter_dimension=0,
        tiled=True,
    )
    joined = lax.psum_scatter(
        jnp.concatenate(
            [
                factor * key_side(lax.axis_size("row") * row_share, score_grad, queries),
                key_side(lax.axis_size("row") * row_share, probabilities, out_grad),
            ],
            axis=1,
        ),
        "row",
        scatter_dimension=0,
        tiled=True,
    )
    key_grad = joined[:, :key_count]
    value_grad = joined[:, key_count:]
    return (
        query_grad.astype(jnp.bfloat16),
        key_grad.astype(jnp.bfloat16),
        value_grad.astype(jnp.bfloat16),
    )


def solution(mesh):
    in_specs = (
        P("row", None),
        P("col", None),
        P("col", None),
        P("row", None),
        P(None, "row"),
        P(),
        P("row"),
        P("col"),
    )
    out_specs = (P("col", "row"), P("row", "col"), P("row", "col"))
    return jax.shard_map(local, mesh=mesh, in_specs=in_specs, out_specs=out_specs, check_vma=False)
```

profile of v0, /device:TPU:1, one launch (start us, length us, event | category | flops | bytes accessed | tf_op | source)
XLA Modules:
  0.0 695.6 jit_solution(3739410599139716831)
XLA Ops:
  8.7 212.9 %while.30 = (s32[]{:T(128)}, bf16[16,512,256]{1,2,0:T(8,128)(2,1)}, f32[16,512]{1,0:T(8,128)}, f32[16,512]{1,0:T(8,128)}, s32[16]{0:T(128)S(1)}, /*index=5*/f32[...) while((s32[]{:T(128)}, bf16[16,512,256]{1,2,0:T(8,128)(2,1)}, ...), condition=%wide.region_3.4_spmd.clone, body=%wide.region_0.3_spmd.clone.sunk | while | flops 68418568 | bytes 2254181 | solution.py:49
  14.7 2.4 fusion.51
  17.2 1.6 fusion.52
  28.0 2.4 fusion.51
  30.5 1.6 fusion.52
  41.3 2.4 fusion.51
  54.6 2.4 fusion.51
  57.1 1.6 fusion.52
  68.0 2.4 fusion.51
  81.3 2.4 fusion.51
  94.6 2.4 fusion.51
  107.9 2.4 fusion.51
  121.2 2.4 fusion.51
  134.5 2.4 fusion.51
  147.8 2.4 fusion.51
  150.2 1.6 fusion.52
  161.1 2.4 fusion.51
  174.4 2.4 fusion.51
  187.7 2.4 fusion.51
  201.0 2.4 fusion.51
  214.3 2.4 fusion.51
  221.7 2.9 copy.19
  224.6 5.0 fusion.33
  229.6 2.9 copy.18
  232.4 112.2 %all-reduce.3.cloned.1.call-done = (f32[16,512]{1,0:T(8,128)}, f32[16,512]{1,0:T(8,128)}) async-done(((f32[16,512]{1,0:T(8,128)}, f32[16,512]{1,0:T(8,128)}), (f32[16,512]{1,0:T(8,128)}, f32[16,512]{1,0:T(8,128)})) %all-reduce.3.cloned.1.call-update) | async-done | bytes 65552 | tf_op jit(solution)/shard_map/psum | solution.py:50
  345.4 140.2 %while.31 = (s32[]{:T(128)}, bf16[16,512,256]{2,1,0:T(8,128)(2,1)}, s32[16]{0:T(128)S(1)}, f32[16]{0:T(128)S(1)}, bf16[512,2048]{1,0:T(8,128)(2,1)}, /*index=5*/...) while((s32[]{:T(128)}, bf16[16,512,256]{2,1,0:T(8,128)(2,1)}, ...), condition=%wide.region_7.8_spmd.clone, body=%wide.region_6.7_spmd.clone.sunk | while | flops 68288520 | bytes 1723205 | solution.py:66
  351.8 2.4 fusion.57
  360.5 2.4 fusion.57
  369.3 2.4 fusion.57
  378.1 2.4 fusion.57
  386.9 2.4 fusion.57
  395.6 2.4 fusion.57
  404.4 2.4 fusion.57
  413.1 2.4 fusion.57
  421.9 2.4 fusion.57
  430.6 2.4 fusion.57
  439.4 2.4 fusion.57
  448.2 2.4 fusion.57
  456.9 2.4 fusion.57
  465.7 2.4 fusion.57
  474.4 2.4 fusion.57
  483.2 2.4 fusion.57
  485.6 3.1 convolution_multiply_fusion.4
  488.7 2.5 pad_maximum_fusion
  492.9 5.6 convolution_multiply_fusion.3
  498.6 87.9 %reduce-scatter.5.cloned.1.call-done = f32[128,512]{1,0:T(8,128)} async-done(((f32[2048,512]{1,0:T(8,128)}), f32[128,512]{1,0:T(8,128)}) %reduce-scatter.5.cloned.1.call-update) | async-done | bytes 262160 | tf_op jit(solution)/shard_map/reduce_scatter | solution.py:78
  588.1 99.4 %reduce-scatter.3.cloned.1.call-done = f32[128,512]{1,0:T(8,128)} async-done(((f32[2048,512]{1,0:T(8,128)}), f32[128,512]{1,0:T(8,128)}) %reduce-scatter.3.cloned.1.call-update) | async-done | bytes 262160 | tf_op jit(solution)/shard_map/reduce_scatter | solution.py:69
  687.5 1.6 convert_element_type.17
  (198 shorter events, 167.5 us)
Async XLA Ops:
  7.2 337.4 %all-reduce.3.cloned.1.call-start = ((), (), s32[]{:S(2)}) async-start(), calls=%async_computation.4 | async-start | bytes 131072 | tf_op jit(solution)/shard_map/psum | solution.py:50
  221.6 364.8 %reduce-scatter.5.cloned.1.call-start = ((), (), s32[]{:S(2)}) async-start(), calls=%async_computation.3 | async-start | bytes 4456448 | tf_op jit(solution)/shard_map/reduce_scatter | solution.py:78
  229.6 115.9 %copy-start.2 = (f32[16]{0:T(128)S(1)}, f32[16]{0:T(128)}, u32[]{:S(2)}) copy-start(f32[16]{0:T(128)} %get-tuple-element.726) | copy-start | bytes 196
  485.6 3.1 copy-start
  491.2 1.2 copy-start.1
  491.2 196.3 %reduce-scatter.3.cloned.1.call-start = ((), (), s32[]{:S(2)}) async-start(), calls=%async_computation.2 | async-start | bytes 4456448 | tf_op jit(solution)/shard_map/reduce_scatter | solution.py:69
Sparse Core Ops, SparseCore 0:
  221.8 122.8 all-reduce.2
  491.3 95.1 reduce-scatter.4
  589.0 98.4 reduce-scatter.2
where the time goes:
time: 704 us; the launch traced here: 696 us
  waiting for transfers between devices  299 us (42%)
  matrix products  134 us (19%)
  local copies, waits for them, and re-layouts  124 us (18%)
  loops' own time  108 us (15%)
  other arithmetic  16.3 us (2%)
  between operations  13.8 us (2%)
    psum x1, waiting for transfers between devices, local(): totals, masses = lax.psum((totals, masses), 'col')  112 us
    reduce_scatter x1, waiting for transfers between devices, local(): lax.psum_scatter(factor * jnp.einsum('hqk,khd->hdq', score_grad, columns,...  99.4 us
    reduce_scatter x1, waiting for transfers between devices, local(): lax.psum_scatter(jnp.concatenate([factor * key_side(lax.axis_size('row')...  87.9 us
    dot_general x32, matrix products, head_parts(): jnp.einsum('qd,kd->qk', query_head, key_head, preferred_element_type=jnp....  77.2 us
    another operation x1, loops' own time, local(): probabilities, totals, masses = lax.map(first_pass, head_ids)  55 us
    another operation x1, loops' own time, local(): score_grad = lax.map(second_pass, head_ids)  52.8 us
    dot_general x32, matrix products, head_parts(): jnp.einsum('qd,kd->qk', grad_head, value_head, preferred_element_type=jnp...  43.4 us
    dynamic_update_slice x32, local copies, waits for them, and re-layouts, local(): probabilities, totals, masses = lax.map(first_pass, head_ids)  43 us
  transfers between devices with their start and end apart: 3, of which 3 were waited for; matrix products, arithmetic and copies ran while one was open for 3% of the time, Pallas kernels for 0%

commit v1 on v0

v1 whole, which is shorter than its diff:
```python
import math

import jax
import jax.numpy as jnp
from jax import lax
from jax.experimental import pallas as pl
from jax.experimental.pallas import tpu as pltpu
from jax.sharding import PartitionSpec as P

MESH = pl.DeviceIdType.MESH
DH = 128
BLK = 128
QN = 512
N = 16
SH = 32
F32 = jnp.float32
BF16 = jnp.bfloat16
FACTOR = 1.0 / math.sqrt(DH)


def dot(a, b):
    return jnp.dot(a, b, preferred_element_type=F32)


def kernel(
    queries, keys, values, out_grad, tau, alpha, query_blocks, key_blocks,
    dq_out, dk_out, dv_out,
    kbuf, vbuf, qh, gh, tau_v, send_k, send_v, blk_s,
    gk, gv, blk,
    qt, gt, w_all, dp_all, probs, tot, mass, dq_acc,
    pk, pv, core_k, core_v, sum_k, sum_v, half_k, half_v, full_k, full_v,
    own_k, own_v, col_k, col_v, row_k, row_v,
    in_sem, a_send, a_recv, y_send, y_recv, m_send, m_recv, c_send, c_recv,
    h_send, h_recv, f_send, f_recv, p_send, p_recv, q_send, q_recv,
):
    r = lax.axis_index("row")
    c = lax.axis_index("col")
    y = r // 4
    xh = (r // 2) % 2
    core = r % 2
    other = 1 - core
    mate = y * 4 + xh * 2 + other
    yp = (y + 1) % 4
    ym = (y + 3) % 4
    yo = (y + 2) % 4
    row_p = yp * 4 + xh * 2 + core
    row_m = ym * 4 + xh * 2 + core
    share = y * 2 + core

    def send(src, dst, ssem, rsem, row, col):
        return pltpu.make_async_remote_copy(
            src_ref=src, dst_ref=dst, send_sem=ssem, recv_sem=rsem,
            device_id=(row, col), device_id_type=MESH,
        )

    loads = [
        pltpu.make_async_copy(keys.at[pl.ds(pl.multiple_of(share * SH, SH), SH), :], kbuf, in_sem.at[0]),
        pltpu.make_async_copy(values.at[pl.ds(pl.multiple_of(share * SH, SH), SH), :], vbuf, in_sem.at[1]),
        pltpu.make_async_copy(queries.at[:, pl.ds(pl.multiple_of(c * DH, DH), DH)], qh, in_sem.at[2]),
        pltpu.make_async_copy(out_grad.at[:, pl.ds(pl.multiple_of(c * DH, DH), DH)], gh, in_sem.at[3]),
        pltpu.make_async_copy(tau, tau_v, in_sem.at[4]),
    ]
    for load in loads:
        load.start()
    barrier = pltpu.get_barrier_semaphore()
    for j in range(1, N):
        pl.semaphore_signal(barrier, inc=1, device_id=(r, (c + j) % N), device_id_type=MESH)
        pl.semaphore_signal(barrier, inc=1, device_id=((r + j) % N, c), device_id_type=MESH)
    kb = [jnp.full((8, DH), key_blocks[i]).astype(F32) for i in range(2)]
    blk_s[...] = jnp.concatenate(kb, axis=0).astype(BF16)
    loads[0].wait()
    for h in range(N):
        send_k[h] = kbuf[:, h * DH : (h + 1) * DH]
    loads[1].wait()
    for h in range(N):
        send_v[h] = vbuf[:, h * DH : (h + 1) * DH]
    pl.semaphore_wait(barrier, 2 * (N - 1))

    def to_col(j):
        peer = (c + j) % N
        return [
            send(send_k.at[peer], gk.at[share, c], a_send.at[0, j], a_recv.at[0, c], r, peer),
            send(blk_s, blk.at[c], a_send.at[1, j], a_recv.at[1, c], r, peer),
            send(send_v.at[peer], gv.at[share, c], a_send.at[2, j], a_recv.at[2, c], r, peer),
        ]

    def from_col(j):
        peer = (c + j) % N
        return [
            send(send_k.at[c], gk.at[share, peer], a_send.at[0, j], a_recv.at[0, peer], r, peer),
            send(blk_s, blk.at[peer], a_send.at[1, j], a_recv.at[1, peer], r, peer),
            send(send_v.at[c], gv.at[share, peer], a_send.at[2, j], a_recv.at[2, peer], r, peer),
        ]

    sent = [to_col(j) for j in range(1, N)]
    for kind in (0, 1, 2):
        for copies in sent:
            copies[kind].start()
    gk[share, c] = send_k[c]
    gv[share, c] = send_v[c]
    blk[c] = blk_s[...]

    for load in loads[2:]:
        load.wait()
    qt[...] = qh[...].T
    gt[...] = gh[...].T
    tot[...] = jnp.zeros_like(tot)
    mass[...] = jnp.zeros_like(mass)
    dq_acc[...] = jnp.zeros_like(dq_acc)
    excess = jnp.full((8, QN), alpha[c]) - 1.0
    scale = excess * FACTOR
    shift_in = jnp.broadcast_to(tau_v[pl.ds(c, 1), :], (8, QN)) * excess
    power = (1.0 - excess) / excess * (1.0 / math.log(2.0))
    lane = lax.broadcasted_iota(jnp.int32, (8, QN), 1)
    qpos = lane % BLK
    for i in range(4):
        qpos = qpos + jnp.where(lane // BLK == i, query_blocks[i] * BLK, 0)
    qpos = qpos.astype(F32)
    bound = [qpos - (lax.broadcasted_iota(jnp.int32, (8, QN), 0) + 8 * i).astype(F32) for i in range(SH // 8)]

    for j in range(1, N):
        came = from_col(j)
        came[0].wait_recv()
        came[1].wait_recv()

    def gather_copies(kind, buf):
        mine = buf.at[share]
        share_p = yp * 2 + core
        share_m = ym * 2 + core
        first = buf.at[share_p, 0 : N // 2]
        second = buf.at[share_m, N // 2 : N]
        far = yo * 2 + core
        out = dict(
            p=send(mine, mine, y_send.at[kind, 0], y_recv.at[kind, 0], row_p, c),
            m=send(mine, mine, y_send.at[kind, 1], y_recv.at[kind, 1], row_m, c),
            fm=send(first, first, y_send.at[kind, 2], y_recv.at[kind, 2], row_m, c),
            fp=send(second, second, y_send.at[kind, 3], y_recv.at[kind, 3], row_p, c),
        )
        for t, s in enumerate((share, share_p, share_m, far)):
            out["mate", t] = send(buf.at[s], buf.at[s], m_send.at[kind, t], m_recv.at[kind, t], mate, c)
        got = dict(
            p=send(buf.at[share_m], buf.at[share_m], y_send.at[kind, 0], y_recv.at[kind, 0], row_m, c),
            m=send(buf.at[share_p], buf.at[share_p], y_send.at[kind, 1], y_recv.at[kind, 1], row_p, c),
            fm=send(buf.at[far, 0 : N // 2], buf.at[far, 0 : N // 2], y_send.at[kind, 2], y_recv.at[kind, 2], row_p, c),
            fp=send(buf.at[far, N // 2 : N], buf.at[far, N // 2 : N], y_send.at[kind, 3], y_recv.at[kind, 3], row_m, c),
        )
        for t, yy in enumerate((y, yp, ym, yo)):
            s = yy * 2 + other
            got["mate", t] = send(buf.at[s], buf.at[s], m_send.at[kind, t], m_recv.at[kind, t], mate, c)
        return out, got

    k_out, k_got = gather_copies(0, gk)
    v_out, v_got = gather_copies(1, gv)
    for key in ("p", "m", ("mate", 0)):
        k_out[key].start()
    for j in range(1, N):
        from_col(j)[2].wait_recv()
    for key in ("p", "m", ("mate", 0)):
        v_out[key].start()

    def first_pass(s):
        k_s = gk[s].reshape(N * SH, DH)
        v_s = gv[s].reshape(N * SH, DH)
        scores = dot(k_s, qt[...])
        dp = dot(v_s, gt[...])
        dp_all[s] = dp
        within = ((s % 4) * SH).astype(F32)
        late = s // 4
        t_sum = jnp.zeros((8, QN), F32)
        m_sum = jnp.zeros((8, QN), F32)
        for j in range(N):
            b16 = blk[j].astype(F32)
            b = jnp.where(late == 0, b16[0:8], b16[8:16]) * BLK + within
            b = jnp.concatenate([b] * (QN // BLK), axis=1)
            for i in range(SH // 8):
                lo = j * SH + i * 8
                x = scores[lo : lo + 8] * scale - shift_in
                x = jnp.where(b <= bound[i], jnp.maximum(x, 0.0), 0.0)
                w = jnp.exp2(jnp.log(x) * power)
                w_all[s, lo : lo + 8, :] = w
                probs[lo : lo + 8, :] = w * x
                t_sum = t_sum + w * dp[lo : lo + 8]
                m_sum = m_sum + w
        tot[...] += t_sum
        mass[...] += m_sum
        pv[s] = dot(probs[...].astype(BF16), gh[...]).astype(BF16).reshape(N, SH, DH)

    def core_copy(kind, part, arrived, yy):
        s = yy * 2 + other
        return send(part.at[s], arrived.at[yy], c_send.at[kind, yy], c_recv.at[kind, yy], mate, c)

    def pass_one(i, carry):
        t = i // 2

        @pl.when(i == 1)
        def _():
            k_got["mate", 0].wait_recv()
            v_got["mate", 0].wait_recv()

        @pl.when(i == 2)
        def _():
            for got, out in ((k_got, k_out), (v_got, v_out)):
                got["m"].wait_recv()
                out["fm"].start()
                out["mate", 1].start()
                got["p"].wait_recv()
                out["fp"].start()
                out["mate", 2].start()

        @pl.when(i == 3)
        def _():
            k_got["mate", 1].wait_recv()
            v_got["mate", 1].wait_recv()

        @pl.when(i == 5)
        def _():
            k_got["mate", 2].wait_recv()
            v_got["mate", 2].wait_recv()

        @pl.when(i == 6)
        def _():
            for got, out in ((k_got, k_out), (v_got, v_out)):
                got["fm"].wait_recv()
                got["fp"].wait_recv()
                out["mate", 3].start()

        @pl.when(i == 7)
        def _():
            k_got["mate", 3].wait_recv()
            v_got["mate", 3].wait_recv()

        yy = (y + t + t // 2 - 2 * (t // 3)) % 4
        half = i % 2
        s = yy * 2 + core + half * (other - core)
        first_pass(s)

        @pl.when(half == 1)
        def _():
            core_copy(1, pv, core_v, yy).start()

        return carry

    lax.fori_loop(0, 8, pass_one, 0)

    def add_core(kind, part, arrived, total, yy):
        core_copy(kind, part, arrived, yy).wait_recv()
        total[yy] = (part[yy * 2 + core].astype(F32) + arrived[yy].astype(F32)).astype(BF16)

    H2 = N // 2

    def half_copies(kind, total, arrived):
        return (
            send(total.at[yo, 0:H2], arrived.at[0], h_send.at[kind, 0], h_recv.at[kind, 0], row_p, c),
            send(total.at[yo, H2:N], arrived.at[1], h_send.at[kind, 1], h_recv.at[kind, 1], row_m, c),
        )

    def full_copies(kind, total, arrived):
        return (
            send(total.at[yp], arrived.at[0], f_send.at[kind, 0], f_recv.at[kind, 0], row_p, c),
            send(total.at[ym], arrived.at[1], f_send.at[kind, 1], f_recv.at[kind, 1], row_m, c),
        )

    def add_half_p(kind, total, arrived):
        half_copies(kind, total, arrived)[0].wait_recv()
        total[yp, 0:H2] = (total[yp, 0:H2].astype(F32) + arrived[0].astype(F32)).astype(BF16)
        full_copies(kind, total, full_k if kind == 0 else full_v)[0].start()

    def add_half_m(kind, total, arrived):
        half_copies(kind, total, arrived)[1].wait_recv()
        total[ym, H2:N] = (total[ym, H2:N].astype(F32) + arrived[1].astype(F32)).astype(BF16)
        full_copies(kind, total, full_k if kind == 0 else full_v)[1].start()

    def col_copy(kind, j, out):
        peer = (c + j) % N
        src, dst = (own_k, col_k) if kind == 0 else (own_v, col_v)
        if out:
            return send(src.at[peer], dst.at[c], p_send.at[kind, j], p_recv.at[kind, c], r, peer)
        return send(src.at[c], dst.at[peer], p_send.at[kind, j], p_recv.at[kind, peer], r, peer)

    def row_copy(kind, j, out):
        peer = (r + j) % N
        src, dst = (col_k, row_k) if kind == 0 else (col_v, row_v)
        if out:
            return send(src.at[peer], dst.at[r], q_send.at[kind, j], q_recv.at[kind, r], peer, c)
        return send(src.at[r], dst.at[peer], q_send.at[kind, j], q_recv.at[kind, peer], peer, c)

    def add_own(kind, total, arrived, own, landed):
        for copy in full_copies(kind, total, arrived):
            copy.wait_recv()
        own[...] = (total[y].astype(F32) + arrived[0].astype(F32) + arrived[1].astype(F32)).astype(BF16)
        for j in range(1, N):
            col_copy(kind, j, True).start()
        landed[c] = own[c]

    def to_rows(kind, landed, final):
        for j in range(1, N):
            col_copy(kind, j, False).wait_recv()
        for j in range(1, N):
            row_copy(kind, j, True).start()
        final[r] = landed[r]

    def finish(kind, final, out, factor):
        for j in range(1, N):
            row_copy(kind, j, False).wait_recv()
        both = final[...].astype(F32).reshape(4, 2, 2, SH, DH)
        both = (both[:, 0] + both[:, 1]).reshape(8 * SH, DH)
        out[...] = (both.T * factor).astype(BF16)

    total_all = jnp.sum(tot[...], axis=0, keepdims=True)
    mass_all = jnp.sum(mass[...], axis=0, keepdims=True)
    row_shift = jnp.broadcast_to(total_all / jnp.maximum(mass_all, 1.0), (8, QN))

    add_core(1, pv, core_v, sum_v, yo)
    for copy in half_copies(1, sum_v, half_v):
        copy.start()
    add_core(1, pv, core_v, sum_v, yp)
    add_core(1, pv, core_v, sum_v, ym)
    add_core(1, pv, core_v, sum_v, y)

    def second_pass(s):
        for j in range(N * SH // 8):
            lo = j * 8
            probs[lo : lo + 8, :] = w_all[s, lo : lo + 8, :] * (dp_all[s, lo : lo + 8, :] - row_shift)
        ds = probs[...].astype(BF16)
        pk[s] = dot(ds, qh[...]).astype(BF16).reshape(N, SH, DH)
        dq_acc[...] += lax.dot_general(
            gk[s].reshape(N * SH, DH), ds, (((0,), (0,)), ((), ())), preferred_element_type=F32
        )

    def pass_two(i, carry):
        t = 3 - i // 2
        yy = (y + t + t // 2 - 2 * (t // 3)) % 4
        half = i % 2
        s = yy * 2 + other + half * (core - other)
        second_pass(s)

        @pl.when(half == 0)
        def _():
            core_copy(0, pk, core_k, yy).start()

        @pl.when(half == 1)
        def _():
            add_core(0, pk, core_k, sum_k, yy)

        @pl.when(i == 1)
        def _():
            for copy in half_copies(0, sum_k, half_k):
                copy.start()
            add_half_p(1, sum_v, half_v)
            add_half_m(1, sum_v, half_v)

        @pl.when(i == 3)
        def _():
            add_half_m(0, sum_k, half_k)

        @pl.when(i == 5)
        def _():
            add_half_p(0, sum_k, half_k)
            add_own(1, sum_v, full_v, own_v, col_v)

        return carry

    lax.fori_loop(0, 8, pass_two, 0)
    add_own(0, sum_k, full_k, own_k, col_k)
    to_rows(1, col_v, row_v)
    dq_out[...] = (dq_acc[...] * FACTOR).astype(BF16)
    to_rows(0, col_k, row_k)
    finish(1, row_v, dv_out, 1.0)
    finish(0, row_k, dk_out, FACTOR)

    for copies in sent:
        for copy in copies:
            copy.wait_send()
    for out in (k_out, v_out):
        for copy in out.values():
            copy.wait_send()
    for kind, part, arrived, total, halves, fulls in (
        (0, pk, core_k, sum_k, half_k, full_k),
        (1, pv, core_v, sum_v, half_v, full_v),
    ):
        for yy in range(4):
            core_copy(kind, part, arrived, yy).wait_send()
        for copy in half_copies(kind, total, halves) + full_copies(kind, total, fulls):
            copy.wait_send()
        for j in range(1, N):
            col_copy(kind, j, True).wait_send()
            row_copy(kind, j, True).wait_send()


def local(queries, keys, values, out_grad, tau, alpha, query_blocks, key_blocks):
    any_ = pl.BlockSpec(memory_space=pl.ANY)
    smem = pl.BlockSpec(memory_space=pltpu.SMEM)
    vmem = pl.BlockSpec(memory_space=pltpu.VMEM)
    V = pltpu.VMEM
    dma = pltpu.SemaphoreType.DMA
    part = (8, N, SH, DH)
    quarter = (4, N, SH, DH)
    return pl.pallas_call(
        kernel,
        out_shape=(
            jax.ShapeDtypeStruct((DH, QN), BF16),
            jax.ShapeDtypeStruct((DH, 2 * BLK), BF16),
            jax.ShapeDtypeStruct((DH, 2 * BLK), BF16),
        ),
        in_specs=[any_] * 5 + [smem] * 3,
        out_specs=(vmem,) * 3,
        scratch_shapes=[
            V((SH, N * DH), BF16), V((SH, N * DH), BF16), V((QN, DH), BF16), V((QN, DH), BF16), V((N, QN), F32),
            V((N, SH, DH), BF16), V((N, SH, DH), BF16), V((16, DH), BF16),
            V(part, BF16), V(part, BF16), V((N, 16, DH), BF16),
            V((DH, QN), BF16), V((DH, QN), BF16), V((8, N * SH, QN), F32), V((8, N * SH, QN), F32), V((N * SH, QN), F32),
            V((8, QN), F32), V((8, QN), F32), V((DH, QN), F32),
            V(part, BF16), V(part, BF16), V(quarter, BF16), V(quarter, BF16), V(quarter, BF16), V(quarter, BF16),
            V((2, N // 2, SH, DH), BF16), V((2, N // 2, SH, DH), BF16), V((2, N, SH, DH), BF16), V((2, N, SH, DH), BF16),
            V((N, SH, DH), BF16), V((N, SH, DH), BF16), V((N, SH, DH), BF16), V((N, SH, DH), BF16), V((N, SH, DH), BF16), V((N, SH, DH), BF16),
            dma((5,)), dma((3, N)), dma((3, N)), dma((2, 4)), dma((2, 4)), dma((2, 4)), dma((2, 4)), dma((2, 4)), dma((2, 4)),
            dma((2, 2)), dma((2, 2)), dma((2, 2)), dma((2, 2)), dma((2, N)), dma((2, N)), dma((2, N)), dma((2, N)),
        ],
        compiler_params=pltpu.CompilerParams(
            collective_id=0, has_side_effects=True, vmem_limit_bytes=48 * 1024 * 1024
        ),
    )(queries, keys, values, out_grad, tau, alpha, query_blocks, key_blocks)


def solution(mesh):
    in_specs = (
        P("row", None), P("col", None), P("col", None), P("row", None),
        P(None, "row"), P(), P("row"), P("col"),
    )
    out_specs = (P("col", "row"), P("row", "col"), P("row", "col"))
    return jax.shard_map(local, mesh=mesh, in_specs=in_specs, out_specs=out_specs, check_vma=False)
```

time: 704 us -> 72.3 us (0.10); the launches traced: 696 us -> 72.1 us
  waiting for transfers between devices: 299 us -> 0 us
  matrix products: 134 us -> 0 us
  local copies, waits for them, and re-layouts: 124 us -> 8.67 us
  loops' own time: 108 us -> 0 us
  Pallas kernels: 0 us -> 62.7 us
  other arithmetic: 16.3 us -> 0 us
  between operations: 13.8 us -> 0.66 us
    reduce_scatter x2 -> x0, waiting for transfers between devices: 187 us -> none  [the longest x1 99.4 us: local(): lax.psum_scatter(factor * jnp.einsum('hqk,khd->hdq', score_grad, columns,...]
    dot_general x67 -> x0, matrix products: 134 us -> none  [the longest x32 77.2 us: head_parts(): jnp.einsum('qd,kd->qk', query_head, key_head, preferred_element_type=jnp....]
    psum x1 -> x0, waiting for transfers between devices: 112 us -> none  [local(): totals, masses = lax.psum((totals, masses), 'col')]
    another operation x2 -> x0, loops' own time: 108 us -> none  [the longest x1 55 us: local(): probabilities, totals, masses = lax.map(first_pass, head_ids)]
    dynamic_slice x96 -> x0, local copies, waits for them, and re-layouts: 72.8 us -> none  [the longest x32 29.8 us: head_parts(): excess = alpha[head] - 1.0]
    pallas_call x0 -> x1, Pallas kernels: none -> 62.7 us  [local(): pl.pallas_call(kernel, out_shape=(jax.ShapeDtypeStruct((DH, QN), BF16), j...]
    dynamic_update_slice x32 -> x0, local copies, waits for them, and re-layouts: 43 us -> none  [local(): probabilities, totals, masses = lax.map(first_pass, head_ids)]
    reduce_sum x16 -> x0, other arithmetic: 8.96 us -> none  [first_pass(): jnp.sum(weights_h, axis=1)]
  transfers between devices with their start and end apart: 3 -> 0, of which waited for: 3 -> 0; matrix products, arithmetic and copies ran while one was open for 3% -> 0% of each run, Pallas kernels for 0% -> 0%
where the time goes in v1:
time: 72.3 us; the launch traced here: 72.1 us
  Pallas kernels  62.7 us (87%)
  local copies, waits for them, and re-layouts  8.67 us (12%)
    pallas_call x1, Pallas kernels, local(): pl.pallas_call(kernel, out_shape=(jax.ShapeDtypeStruct((DH, QN), BF16), j...  62.7 us
    unnamed x17, local copies, waits for them, and re-layouts  8.67 us

profile of v1, /device:TPU:1, one launch (start us, length us, event | category | flops | bytes accessed | tf_op | source)
XLA Modules:
  0.0 72.1 jit_solution(4645332792164435318)
XLA Ops:
  0.6 0.0 copy-start
  0.6 1.6 %copy-done = bf16[512,2048]{1,0:T(8,128)(2,1)S(1)} copy-done((bf16[512,2048]{1,0:T(8,128)(2,1)S(1)}, bf16[512,2048]{1,0:T(8,128)(2,1)}, u32[]{:S(2)}) %copy-start) | copy-done | bytes 2097176
  2.2 0.0 copy-start.1
  2.2 1.2 %copy-done.1 = bf16[256,2048]{1,0:T(8,128)(2,1)S(1)} copy-done((bf16[256,2048]{1,0:T(8,128)(2,1)S(1)}, bf16[256,2048]{1,0:T(8,128)(2,1)}, u32[]{:S(2)}) %copy-start.1) | copy-done | bytes 1048600
  3.5 0.0 copy-start.2
  3.5 1.2 %copy-done.2 = bf16[256,2048]{1,0:T(8,128)(2,1)S(1)} copy-done((bf16[256,2048]{1,0:T(8,128)(2,1)S(1)}, bf16[256,2048]{1,0:T(8,128)(2,1)}, u32[]{:S(2)}) %copy-start.2) | copy-done | bytes 1048600
  4.7 0.0 copy-start.3
  4.7 0.8 %copy-done.3 = f32[16,512]{1,0:T(8,128)S(1)} copy-done((f32[16,512]{1,0:T(8,128)S(1)}, f32[16,512]{1,0:T(8,128)}, u32[]{:S(2)}) %copy-start.3) | copy-done | bytes 32792
  5.4 0.0 copy-start.4
  5.4 0.7 copy-done.4
  6.1 0.0 copy-start.5
  6.1 0.7 copy-done.5
  6.7 0.0 copy-start.6
  6.7 0.7 copy-done.6
  7.4 62.7 %shard_map.103 = (bf16[128,512]{1,0:T(8,128)(2,1)S(1)}, bf16[128,256]{1,0:T(8,128)(2,1)S(1)}, bf16[128,256]{1,0:T(8,128)(2,1)S(1)}) custom-call(bf16[512,2048]{1,0:T(8,128)(2,1)S(1)} %copy-done, bf16[256,2048]{1,0:T(8,128)(2,1)S(1)} %copy-done.1, bf16[256,2048]{1,0:T(8,128)(2,1)S(1)} %copy-done.2, bf16[512,2048]{1,0:T(8,128)(2,1)} %out_grad.1, ...), custom_call_target="tpu_custom_call" | custom-call | tf_op jit(solution)/shard_map/pallas_call | solution.py:398
  70.1 0.7 copy.14
  70.8 0.6 copy.15
  71.4 0.6 copy.16
Async XLA Ops:
  0.6 1.6 %copy-start = (bf16[512,2048]{1,0:T(8,128)(2,1)S(1)}, bf16[512,2048]{1,0:T(8,128)(2,1)}, u32[]{:S(2)}) copy-start(bf16[512,2048]{1,0:T(8,128)(2,1)} %queries.1) | copy-start | bytes 6291460
  2.2 1.2 %copy-start.1 = (bf16[256,2048]{1,0:T(8,128)(2,1)S(1)}, bf16[256,2048]{1,0:T(8,128)(2,1)}, u32[]{:S(2)}) copy-start(bf16[256,2048]{1,0:T(8,128)(2,1)} %keys.1) | copy-start | bytes 3145732
  3.5 1.2 %copy-start.2 = (bf16[256,2048]{1,0:T(8,128)(2,1)S(1)}, bf16[256,2048]{1,0:T(8,128)(2,1)}, u32[]{:S(2)}) copy-start(bf16[256,2048]{1,0:T(8,128)(2,1)} %values.1) | copy-start | bytes 3145732
  4.7 0.8 %copy-start.3 = (f32[16,512]{1,0:T(8,128)S(1)}, f32[16,512]{1,0:T(8,128)}, u32[]{:S(2)}) copy-start(f32[16,512]{1,0:T(8,128)} %tau.1) | copy-start | bytes 98308
  5.4 0.7 copy-start.4
  6.1 0.7 copy-start.5
  6.7 0.7 copy-start.6

commit v2 on v0

v2 whole, which is shorter than its diff:
```python
import math

import jax
import jax.numpy as jnp
from jax import lax
from jax.experimental import pallas as pl
from jax.experimental.pallas import tpu as pltpu
from jax.sharding import PartitionSpec as P

MESH = pl.DeviceIdType.MESH
DH = 128
BLK = 128
QN = 512
N = 16
SH = 32
KN = N * SH
M = 8
F32 = jnp.float32
BF16 = jnp.bfloat16
FACTOR = 1.0 / math.sqrt(DH)


def dot(a, b):
    return jnp.dot(a, b, preferred_element_type=F32)


def dot_nt(a, b):
    return lax.dot_general(a, b, (((1,), (1,)), ((), ())), preferred_element_type=F32)


def place(t):
    return t + t // 2 - 2 * (t // 3)


def kernel(
    queries, keys, values, out_grad, tau_in, alpha_in, query_blocks_in, key_blocks_in,
    dq_out, dk_out, dv_out,
    alpha, query_blocks, key_blocks, tau,
    gk, gv, gb, gb_send,
    gq, gg, info,
    kt, w_all, dp_all, probs, dv_acc, dk_acc, stats, stats_in, shifts,
    dq_mine, dq_mate_out, dq_mate_in, dq_sum, dq_in, own_k, own_v, row_k, row_v,
    in_sem, a_send, a_recv, y_send, y_recv, m_send, m_recv, i_send, i_recv, s_send, s_recv,
    c_send, c_recv, d_send, d_recv, p_send, p_recv,
):
    r = lax.axis_index("row")
    c = lax.axis_index("col")
    y = r // 4
    xh = (r // 2) % 2
    core = r % 2
    other = 1 - core
    share = y * 2 + core

    def row_of(yy, cc):
        return yy * 4 + xh * 2 + cc

    mate = row_of(y, other)

    def send(src, dst, ssem, rsem, row, col):
        return pltpu.make_async_remote_copy(
            src_ref=src, dst_ref=dst, send_sem=ssem, recv_sem=rsem,
            device_id=(row, col), device_id_type=MESH,
        )

    def member(j):
        yy = (y + j // 2) % 4
        cc = (core + j) % 2
        return yy, cc, yy * 2 + cc

    barrier = pltpu.get_barrier_semaphore()

    def greet(row, col):
        pl.semaphore_signal(barrier, inc=1, device_id=(row, col), device_id_type=MESH)

    for j in range(1, N):
        greet(r, (c + j) % N)
    for j in range(1, M):
        yy, cc, _ = member(j)
        greet(row_of(yy, cc), c)
    for j in range(1, N):
        greet((r + j) % N, r)

    @pl.when(c != r)
    def _():
        greet(r, r)

    key_rows = pl.ds(pl.multiple_of(share * SH, SH), SH)

    def head(h):
        return pl.ds(pl.multiple_of(h * DH, DH), DH)

    loads = [
        pltpu.make_async_copy(key_blocks_in, key_blocks, in_sem.at[0]),
        pltpu.make_async_copy(query_blocks_in, query_blocks, in_sem.at[1]),
        pltpu.make_async_copy(alpha_in, alpha, in_sem.at[2]),
        pltpu.make_async_copy(tau_in, tau, in_sem.at[3]),
        pltpu.make_async_copy(queries.at[:, head(c)], gq.at[share], in_sem.at[4]),
        pltpu.make_async_copy(out_grad.at[:, head(c)], gg.at[share], in_sem.at[5]),
        pltpu.make_async_copy(keys.at[key_rows, head(c)], gk.at[c], in_sem.at[6]),
        pltpu.make_async_copy(values.at[key_rows, head(c)], gv.at[c], in_sem.at[7]),
    ]
    for load in loads:
        load.start()
    for load in loads[:4]:
        load.wait()
    base = (key_blocks[share // 4] * BLK + (share % 4) * SH).astype(F32)
    gb_send[...] = jnp.full((8, DH), base)
    gb[c] = gb_send[...]
    line = tau[pl.ds(c, 1), :]
    for i in range(4):
        info[share, i : i + 1, :] = line[:, i * DH : (i + 1) * DH]
        info[share, 4 + i : 5 + i, :] = jnp.full((1, DH), query_blocks[i] * BLK).astype(F32)
    for load in loads[4:6]:
        load.wait()

    apart = ((c + N - r) % N + N - 1) // N
    pl.semaphore_wait(barrier, (N - 1) + (M - 1) + (N - 1) + apart)

    def y_copy(kind, buf, t, out):
        step = (1, 3, 2)[t - 1]
        to = row_of((y + step) % 4, core)
        frm_y = (y + 4 - step) % 4
        frm = frm_y * 2 + core
        if out:
            return send(buf.at[share], buf.at[share], y_send.at[kind, t - 1], y_recv.at[kind, t - 1], to, c)
        return send(buf.at[frm], buf.at[frm], y_send.at[kind, t - 1], y_recv.at[kind, t - 1], row_of(frm_y, core), c)

    def mate_copy(kind, buf, t, out):
        yy = (y + 4 - (0, 1, 3, 2)[t]) % 4
        m = yy * 2 + (core if out else other)
        return send(buf.at[m], buf.at[m], m_send.at[kind, t], m_recv.at[kind, t], mate, c)

    both = ((0, gq), (1, gg))
    for t in (1, 2):
        for kind, buf in both:
            y_copy(kind, buf, t, True).start()

    def col_copy(kind, j, out):
        peer = (c + j) % N
        frm = c if out else peer
        src, dst = (
            (keys.at[key_rows, head(peer)], gk.at[frm]),
            (values.at[key_rows, head(peer)], gv.at[frm]),
            (gb_send, gb.at[frm]),
        )[kind]
        return send(src, dst, a_send.at[kind, j], a_recv.at[kind, frm], r, peer)

    far_first = sorted(range(1, N), key=lambda j: -min(j, N - j))
    for kind in (0, 1):
        for j in far_first:
            col_copy(kind, j, True).start()
    for kind, buf in both:
        y_copy(kind, buf, 3, True).start()
    for kind, buf in both:
        mate_copy(kind, buf, 0, True).start()
    for j in far_first:
        col_copy(2, j, True).start()

    def info_copy(j, out):
        yy, cc, m = member(j)
        frm = share if out else m
        return send(info.at[frm], info.at[frm], i_send.at[m], i_recv.at[frm], row_of(yy, cc), c)

    for j in range(1, M):
        info_copy(j, True).start()

    dv_acc[...] = jnp.zeros_like(dv_acc)
    dk_acc[...] = jnp.zeros_like(dk_acc)
    excess = jnp.full((8, QN), alpha[c]) - 1.0
    scale = excess * FACTOR
    power = (1.0 - excess) / excess * (1.0 / math.log(2.0))
    lane = lax.broadcasted_iota(jnp.int32, (8, QN), 1) % BLK
    row8 = lax.broadcasted_iota(jnp.int32, (8, QN), 0)
    ahead = (lane - row8).astype(F32)

    def wide(tile, lo):
        line = jnp.concatenate([tile[lo + i : lo + i + 1, :] for i in range(4)], axis=1)
        return jnp.broadcast_to(line, (8, QN))

    for t in (1, 2):
        for kind, buf in both:
            y_copy(kind, buf, t, False).wait_recv()
            mate_copy(kind, buf, t, True).start()
    for j in range(1, M):
        info_copy(j, False).wait_recv()
    for load in loads[6:]:
        load.wait()
    for kind in (0, 1, 2):
        for j in far_first:
            col_copy(kind, j, False).wait_recv()
    kt[...] = gk[...].reshape(KN, DH).T

    def first_pass(m, place_in_order):
        scores = dot_nt(gk[...].reshape(KN, DH), gq[m])
        dp = dot_nt(gv[...].reshape(KN, DH), gg[m])
        dp_all[m] = dp
        tile = info[m]
        shift_in = wide(tile, 0) * excess
        query = wide(tile, 4) + ahead
        t_sum = jnp.zeros((8, QN), F32)
        m_sum = jnp.zeros((8, QN), F32)
        for j in range(N):
            b = jnp.concatenate([gb[j]] * (QN // DH), axis=1)
            for i in range(SH // 8):
                lo = j * SH + i * 8
                x = scores[lo : lo + 8] * scale - shift_in
                x = jnp.where(b + 8.0 * i <= query, jnp.maximum(x, 0.0), 0.0)
                w = jnp.exp2(jnp.log(x) * power)
                w_all[m, lo : lo + 8, :] = w
                probs[lo : lo + 8, :] = w * x
                t_sum = t_sum + w * dp[lo : lo + 8]
                m_sum = m_sum + w
        dv_acc[...] += dot(probs[...].astype(BF16), gg[m])
        t_sum = jnp.sum(t_sum, axis=0, keepdims=True)
        m_sum = jnp.sum(m_sum, axis=0, keepdims=True)
        parts = [s[:, i * DH : (i + 1) * DH] for s in (t_sum, m_sum) for i in range(4)]
        stats[place_in_order] = jnp.concatenate(parts, axis=0)

    BATCH = ((0, 6), (6, 8))

    def stats_copy(batch, j, out):
        yy, cc, m = member(j)
        frm = share if out else m
        lo, hi = BATCH[batch]
        return send(
            stats.at[lo:hi], stats_in.at[frm, lo:hi], s_send.at[batch, m], s_recv.at[batch, frm], row_of(yy, cc), c
        )

    def pass_one(i, carry):
        @pl.when(i == 1)
        def _():
            for kind, buf in both:
                mate_copy(kind, buf, 0, False).wait_recv()

        @pl.when(i == 3)
        def _():
            for kind, buf in both:
                mate_copy(kind, buf, 1, False).wait_recv()

        @pl.when(i == 4)
        def _():
            for kind, buf in both:
                y_copy(kind, buf, 3, False).wait_recv()
                mate_copy(kind, buf, 3, True).start()

        @pl.when(i == 5)
        def _():
            for kind, buf in both:
                mate_copy(kind, buf, 2, False).wait_recv()

        @pl.when(i == 7)
        def _():
            for kind, buf in both:
                mate_copy(kind, buf, 3, False).wait_recv()

        yy = (y + 4 - place(i // 2)) % 4
        first_pass(yy * 2 + (core + i) % 2, i)

        @pl.when(i == 5)
        def _():
            for j in range(1, M):
                stats_copy(0, j, True).start()

        return carry

    lax.fori_loop(0, M, pass_one, 0)
    for j in range(1, M):
        stats_copy(1, j, True).start()

    def last_copy(kind, j, out):
        src, dst = ((own_k, row_k), (own_v, row_v))[kind]
        if out:
            peer = (c + j) % N
            return send(src.at[peer], dst.at[r], p_send.at[kind, j], p_recv.at[kind, r], c, peer)
        peer = (r + j) % N
        return send(src.at[c], dst.at[peer], p_send.at[kind, j], p_recv.at[kind, peer], peer, r)

    def send_last(kind, total):
        src, dst = ((own_k, row_k), (own_v, row_v))[kind]
        src[...] = total.astype(BF16).reshape(N, SH, DH)
        for j in range(1, N):
            last_copy(kind, j, True).start()

        @pl.when(c != r)
        def _():
            last_copy(kind, 0, True).start()

        @pl.when(c == r)
        def _():
            dst[r] = src[c]

    def finish(kind, out, factor):
        for j in range(1, N):
            last_copy(kind, j, False).wait_recv()

        @pl.when(c != r)
        def _():
            last_copy(kind, 0, False).wait_recv()

        final = (row_k, row_v)[kind]
        pairs = final[...].astype(F32).reshape(4, 2, 2, SH, DH)
        pairs = (pairs[:, 0] + pairs[:, 1]).reshape(M * SH, DH)
        out[...] = (pairs.T * factor).astype(BF16)

    send_last(1, dv_acc[...])

    for batch in (0, 1):
        for j in range(1, M):
            stats_copy(batch, j, False).wait_recv()
    stats_in[share] = stats[...]

    def one_shift(m, carry):
        total = jnp.zeros((8, DH), F32)
        for src in range(M):
            back = place((src // 2 + 4 - m // 2) % 4)
            total = total + stats_in[src, back * 2 + (src + m) % 2]
        shift = total[0:4] / jnp.maximum(total[4:8], 1.0)
        shifts[m] = wide(shift, 0)
        return carry

    lax.fori_loop(0, M, one_shift, 0)

    def second_pass(m):
        row_shift = shifts[m]
        for j in range(KN // 8):
            lo = j * 8
            probs[lo : lo + 8, :] = w_all[m, lo : lo + 8, :] * (dp_all[m, lo : lo + 8, :] - row_shift)
        ds = probs[...].astype(BF16)
        dk_acc[...] += dot(ds, gq[m])
        return dot(kt[...], ds)

    def core_copy(yy):
        return send(dq_mate_out.at[yy], dq_mate_in.at[yy], c_send.at[yy], c_recv.at[yy], mate, c)

    def dq_copy(t, out):
        step = (1, 3, 2)[t - 1]
        to_y = (y + 4 - step) % 4
        if out:
            return send(dq_sum.at[to_y], dq_in.at[t - 1], d_send.at[t - 1], d_recv.at[t - 1], row_of(to_y, core), c)
        frm_y = (y + step) % 4
        return send(dq_sum.at[y], dq_in.at[t - 1], d_send.at[t - 1], d_recv.at[t - 1], row_of(frm_y, core), c)

    def add_mate(t):
        yy = (y + 4 - (0, 1, 3, 2)[t]) % 4
        core_copy(yy).wait_recv()
        dq_sum[yy] = (dq_mine[yy] + dq_mate_in[yy].astype(F32)).astype(BF16)
        if t:
            dq_copy(t, True).start()

    def pass_two(i, carry):
        yy = (y + 4 - place(3 - i // 2)) % 4
        part = second_pass(yy * 2 + (other + i) % 2)

        @pl.when(i % 2 == 0)
        def _():
            dq_mate_out[yy] = part.astype(BF16)
            core_copy(yy).start()

        @pl.when(i % 2 == 1)
        def _():
            dq_mine[yy] = part

        @pl.when(i == 3)
        def _():
            add_mate(3)

        @pl.when(i == 5)
        def _():
            add_mate(2)

        return carry

    lax.fori_loop(0, M, pass_two, 0)
    send_last(0, dk_acc[...])
    add_mate(1)
    add_mate(0)
    finish(1, dv_out, 1.0)
    dq = dq_sum[y].astype(F32)
    for t in (3, 2, 1):
        dq_copy(t, False).wait_recv()
        dq = dq + dq_in[t - 1].astype(F32)
    dq_out[...] = (dq * FACTOR).astype(BF16)
    finish(0, dk_out, FACTOR)

    for kind, buf in both:
        for t in (1, 2, 3):
            y_copy(kind, buf, t, True).wait_send()
        for t in range(4):
            mate_copy(kind, buf, t, True).wait_send()
    for kind in (0, 1, 2):
        for j in far_first:
            col_copy(kind, j, True).wait_send()
    for j in range(1, M):
        info_copy(j, True).wait_send()
        stats_copy(0, j, True).wait_send()
        stats_copy(1, j, True).wait_send()
    for yy in range(4):
        core_copy(yy).wait_send()
    for t in (1, 2, 3):
        dq_copy(t, True).wait_send()
    for kind in (0, 1):
        for j in range(1, N):
            last_copy(kind, j, True).wait_send()

    @pl.when(c != r)
    def _():
        for kind in (0, 1):
            last_copy(kind, 0, True).wait_send()


def local(*args):
    hbm = pl.BlockSpec(memory_space=pltpu.HBM)
    vmem = pl.BlockSpec(memory_space=pltpu.VMEM)
    V = pltpu.VMEM
    S = pltpu.SMEM
    dma = pltpu.SemaphoreType.DMA
    return pl.pallas_call(
        kernel,
        out_shape=(
            jax.ShapeDtypeStruct((DH, QN), BF16),
            jax.ShapeDtypeStruct((DH, 2 * BLK), BF16),
            jax.ShapeDtypeStruct((DH, 2 * BLK), BF16),
        ),
        in_specs=[hbm] * 8,
        out_specs=(vmem,) * 3,
        scratch_shapes=[
            S((N,), F32), S((4,), jnp.int32), S((2,), jnp.int32), V((N, QN), F32),
            V((N, SH, DH), BF16), V((N, SH, DH), BF16), V((N, 8, DH), F32), V((8, DH), F32),
            V((M, QN, DH), BF16), V((M, QN, DH), BF16), V((M, 8, DH), F32),
            V((DH, KN), BF16), V((M, KN, QN), F32), V((M, KN, QN), F32), V((KN, QN), F32),
            V((KN, DH), F32), V((KN, DH), F32), V((M, 8, DH), F32), V((M, M, 8, DH), F32), V((M, 8, QN), F32),
            V((4, DH, QN), F32), V((4, DH, QN), BF16), V((4, DH, QN), BF16), V((4, DH, QN), BF16), V((3, DH, QN), BF16),
            V((N, SH, DH), BF16), V((N, SH, DH), BF16), V((N, SH, DH), BF16), V((N, SH, DH), BF16),
            dma((8,)), dma((3, N)), dma((3, N)), dma((2, 3)), dma((2, 3)), dma((2, 4)), dma((2, 4)),
            dma((M,)), dma((M,)), dma((2, M)), dma((2, M)),
            dma((4,)), dma((4,)), dma((3,)), dma((3,)), dma((2, N)), dma((2, N)),
        ],
        compiler_params=pltpu.CompilerParams(
            collective_id=0, has_side_effects=True, vmem_limit_bytes=48 * 1024 * 1024
        ),
    )(*[pltpu.with_memory_space_constraint(a, pltpu.HBM) for a in args])


def solution(mesh):
    in_specs = (
        P("row", None), P("col", None), P("col", None), P("row", None),
        P(None, "row"), P(), P("row"), P("col"),
    )
    out_specs = (P("col", "row"), P("row", "col"), P("row", "col"))
    return jax.shard_map(local, mesh=mesh, in_specs=in_specs, out_specs=out_specs, check_vma=False)
```

time: 704 us -> 54.7 us (0.08); the launches traced: 696 us -> 54.2 us
  waiting for transfers between devices: 299 us -> 0 us
  matrix products: 134 us -> 0 us
  local copies, waits for them, and re-layouts: 124 us -> 1.92 us
  loops' own time: 108 us -> 0 us
  Pallas kernels: 0 us -> 51.7 us
  other arithmetic: 16.3 us -> 0 us
  between operations: 13.8 us -> 0.64 us
    reduce_scatter x2 -> x0, waiting for transfers between devices: 187 us -> none  [the longest x1 99.4 us: local(): lax.psum_scatter(factor * jnp.einsum('hqk,khd->hdq', score_grad, columns,...]
    dot_general x67 -> x0, matrix products: 134 us -> none  [the longest x32 77.2 us: head_parts(): jnp.einsum('qd,kd->qk', query_head, key_head, preferred_element_type=jnp....]
    psum x1 -> x0, waiting for transfers between devices: 112 us -> none  [local(): totals, masses = lax.psum((totals, masses), 'col')]
    another operation x2 -> x0, loops' own time: 108 us -> none  [the longest x1 55 us: local(): probabilities, totals, masses = lax.map(first_pass, head_ids)]
    dynamic_slice x96 -> x0, local copies, waits for them, and re-layouts: 72.8 us -> none  [the longest x32 29.8 us: head_parts(): excess = alpha[head] - 1.0]
    pallas_call x0 -> x1, Pallas kernels: none -> 51.7 us  [local(): pl.pallas_call(kernel, out_shape=(jax.ShapeDtypeStruct((DH, QN), BF16), j...]
    dynamic_update_slice x32 -> x0, local copies, waits for them, and re-layouts: 43 us -> none  [local(): probabilities, totals, masses = lax.map(first_pass, head_ids)]
    reduce_sum x16 -> x0, other arithmetic: 8.96 us -> none  [first_pass(): jnp.sum(weights_h, axis=1)]
  transfers between devices with their start and end apart: 3 -> 0, of which waited for: 3 -> 0; matrix products, arithmetic and copies ran while one was open for 3% -> 0% of each run, Pallas kernels for 0% -> 0%
where the time goes in v2:
time: 54.7 us; the launch traced here: 54.2 us
  Pallas kernels  51.7 us (95%)
  local copies, waits for them, and re-layouts  1.92 us (4%)
  between operations  0.64 us (1%)
    pallas_call x1, Pallas kernels, local(): pl.pallas_call(kernel, out_shape=(jax.ShapeDtypeStruct((DH, QN), BF16), j...  51.7 us
    unnamed x3, local copies, waits for them, and re-layouts  1.92 us

profile of v2, /device:TPU:1, one launch (start us, length us, event | category | flops | bytes accessed | tf_op | source)
XLA Modules:
  0.0 54.2 jit_solution(16121721418596177477)
XLA Ops:
  0.6 51.7 %shard_map.103 = (bf16[128,512]{1,0:T(8,128)(2,1)S(1)}, bf16[128,256]{1,0:T(8,128)(2,1)S(1)}, bf16[128,256]{1,0:T(8,128)(2,1)S(1)}) custom-call(bf16[512,2048]{1,0:T(8,128)(2,1)} %queries.1, bf16[256,2048]{1,0:T(8,128)(2,1)} %keys.1, bf16[256,2048]{1,0:T(8,128)(2,1)} %values.1, bf16[512,2048]{1,0:T(8,128)(2,1)} %out_grad.1, f32[16,512]{1,0:T(8,128)} %tau_in.1, ...), custom_call_target="tpu_custom_call" | custom-call | tf_op jit(solution)/shard_map/pallas_call | solution.py:417
  52.3 0.7 %copy.14 = bf16[128,512]{1,0:T(8,128)(2,1)} copy(bf16[128,512]{1,0:T(8,128)(2,1)S(1)} %get-tuple-element.6) | data formatting | bytes 262144
  53.0 0.6 %copy.15 = bf16[128,256]{1,0:T(8,128)(2,1)} copy(bf16[128,256]{1,0:T(8,128)(2,1)S(1)} %get-tuple-element.7) | data formatting | bytes 131072
  53.6 0.6 %copy.16 = bf16[128,256]{1,0:T(8,128)(2,1)} copy(bf16[128,256]{1,0:T(8,128)(2,1)S(1)} %get-tuple-element.8) | data formatting | bytes 131072

commit v3 on v2

--- a/solution.py
+++ b/solution.py
@@ -101,39 +101,8 @@
     ]
     for load in loads:
         load.start()
-    for load in loads[:4]:
-        load.wait()
-    base = (key_blocks[share // 4] * BLK + (share % 4) * SH).astype(F32)
-    gb_send[...] = jnp.full((8, DH), base)
-    gb[c] = gb_send[...]
-    line = tau[pl.ds(c, 1), :]
-    for i in range(4):
-        info[share, i : i + 1, :] = line[:, i * DH : (i + 1) * DH]
-        info[share, 4 + i : 5 + i, :] = jnp.full((1, DH), query_blocks[i] * BLK).astype(F32)
-    for load in loads[4:6]:
-        load.wait()
-
     apart = ((c + N - r) % N + N - 1) // N
     pl.semaphore_wait(barrier, (N - 1) + (M - 1) + (N - 1) + apart)
-
-    def y_copy(kind, buf, t, out):
-        step = (1, 3, 2)[t - 1]
-        to = row_of((y + step) % 4, core)
-        frm_y = (y + 4 - step) % 4
-        frm = frm_y * 2 + core
-        if out:
-            return send(buf.at[share], buf.at[share], y_send.at[kind, t - 1], y_recv.at[kind, t - 1], to, c)
-        return send(buf.at[frm], buf.at[frm], y_send.at[kind, t - 1], y_recv.at[kind, t - 1], row_of(frm_y, core), c)
-
-    def mate_copy(kind, buf, t, out):
-        yy = (y + 4 - (0, 1, 3, 2)[t]) % 4
-        m = yy * 2 + (core if out else other)
-        return send(buf.at[m], buf.at[m], m_send.at[kind, t], m_recv.at[kind, t], mate, c)
-
-    both = ((0, gq), (1, gg))
-    for t in (1, 2):
-        for kind, buf in both:
-            y_copy(kind, buf, t, True).start()
 
     def col_copy(kind, j, out):
         peer = (c + j) % N
@@ -146,23 +115,64 @@
         return send(src, dst, a_send.at[kind, j], a_recv.at[kind, frm], r, peer)
 
     far_first = sorted(range(1, N), key=lambda j: -min(j, N - j))
-    for kind in (0, 1):
-        for j in far_first:
-            col_copy(kind, j, True).start()
-    for kind, buf in both:
-        y_copy(kind, buf, 3, True).start()
-    for kind, buf in both:
-        mate_copy(kind, buf, 0, True).start()
-    for j in far_first:
-        col_copy(2, j, True).start()
+
+    both = ((0, gq), (1, gg))
+    own = (queries, out_grad)
+    HALF = (pl.ds(0, QN // 2), pl.ds(QN // 2, QN // 2))
+
+    def y_copy(kind, way, stage, out):
+        buf = both[kind][1]
+        step = 1 if way == 0 else 3
+        part = HALF[way] if stage != 1 else HALF[1 - way]
+        sem = (kind, way, stage)
+        back = (1 if stage < 2 else 2) * (4 - step)
+        if out and stage == 2:
+            m = ((y + 4 - step) % 4) * 2 + core
+        else:
+            m = share if out else ((y + back) % 4) * 2 + core
+        dst = buf.at[m, part]
+        src = own[kind].at[part, head(c)] if out and stage < 2 else dst
+        peer = (y + step) % 4 if out else (y + 4 - step) % 4
+        return send(src, dst, y_send.at[sem], y_recv.at[sem], row_of(peer, core), c)
+
+    def mate_copy(kind, t, part, out):
+        buf = both[kind][1]
+        yy = (y + 4 - (0, 1, 3, 2)[t]) % 4
+        dst = buf.at[yy * 2 + (core if out else other), HALF[part]]
+        src = own[kind].at[HALF[part], head(c)] if out and t == 0 else dst
+        return send(src, dst, m_send.at[kind, t, part], m_recv.at[kind, t, part], mate, c)
 
     def info_copy(j, out):
         yy, cc, m = member(j)
         frm = share if out else m
         return send(info.at[frm], info.at[frm], i_send.at[m], i_recv.at[frm], row_of(yy, cc), c)
 
+    for j in far_first:
+        col_copy(0, j, True).start()
+    for kind in (0, 1):
+        for way in (0, 1):
+            y_copy(kind, way, 0, True).start()
+    for load in loads[:4]:
+        load.wait()
+    base = (key_blocks[share // 4] * BLK + (share % 4) * SH).astype(F32)
+    gb_send[...] = jnp.full((1, DH), base)
+    gb[c] = gb_send[...]
+    line = tau[pl.ds(c, 1), :]
+    for i in range(4):
+        info[share, i : i + 1, :] = line[:, i * DH : (i + 1) * DH]
+        info[share, 4 + i : 5 + i, :] = jnp.full((1, DH), query_blocks[i] * BLK).astype(F32)
+    for j in far_first:
+        col_copy(2, j, True).start()
     for j in range(1, M):
         info_copy(j, True).start()
+    for j in far_first:
+        col_copy(1, j, True).start()
+    for kind in (0, 1):
+        for way in (0, 1):
+            y_copy(kind, way, 1, True).start()
+    for kind in (0, 1):
+        for part in (0, 1):
+            mate_copy(kind, 0, part, True).start()
 
     dv_acc[...] = jnp.zeros_like(dv_acc)
     dk_acc[...] = jnp.zeros_like(dk_acc)
@@ -177,44 +187,63 @@
         line = jnp.concatenate([tile[lo + i : lo + i + 1, :] for i in range(4)], axis=1)
         return jnp.broadcast_to(line, (8, QN))
 
-    for t in (1, 2):
-        for kind, buf in both:
-            y_copy(kind, buf, t, False).wait_recv()
-            mate_copy(kind, buf, t, True).start()
+    def arrived(way, stage):
+        t = (3 if stage == 2 else 1 + way)
+        part = way if stage != 1 else 1 - way
+        for kind in (0, 1):
+            y_copy(kind, way, stage, False).wait_recv()
+            if stage == 0:
+                y_copy(kind, way, 2, True).start()
+            mate_copy(kind, t, part, True).start()
+
+    def from_mate(t):
+        for kind in (0, 1):
+            for part in (0, 1):
+                mate_copy(kind, t, part, False).wait_recv()
+
+    for load in loads[4:]:
+        load.wait()
+    for way in (0, 1):
+        arrived(way, 0)
     for j in range(1, M):
         info_copy(j, False).wait_recv()
-    for load in loads[6:]:
-        load.wait()
-    for kind in (0, 1, 2):
+    for kind in (0, 2):
         for j in far_first:
             col_copy(kind, j, False).wait_recv()
     kt[...] = gk[...].reshape(KN, DH).T
 
-    def first_pass(m, place_in_order):
+    def lines(total):
+        total = jnp.sum(total, axis=0, keepdims=True)
+        return jnp.concatenate([total[:, i * DH : (i + 1) * DH] for i in range(4)], axis=0)
+
+    def weigh(m, spot):
         scores = dot_nt(gk[...].reshape(KN, DH), gq[m])
-        dp = dot_nt(gv[...].reshape(KN, DH), gg[m])
-        dp_all[m] = dp
         tile = info[m]
         shift_in = wide(tile, 0) * excess
         query = wide(tile, 4) + ahead
-        t_sum = jnp.zeros((8, QN), F32)
         m_sum = jnp.zeros((8, QN), F32)
         for j in range(N):
-            b = jnp.concatenate([gb[j]] * (QN // DH), axis=1)
-            for i in range(SH // 8):
-                lo = j * SH + i * 8
-                x = scores[lo : lo + 8] * scale - shift_in
-                x = jnp.where(b + 8.0 * i <= query, jnp.maximum(x, 0.0), 0.0)
-                w = jnp.exp2(jnp.log(x) * power)
-                w_all[m, lo : lo + 8, :] = w
-                probs[lo : lo + 8, :] = w * x
-                t_sum = t_sum + w * dp[lo : lo + 8]
-                m_sum = m_sum + w
-        dv_acc[...] += dot(probs[...].astype(BF16), gg[m])
-        t_sum = jnp.sum(t_sum, axis=0, keepdims=True)
-        m_sum = jnp.sum(m_sum, axis=0, keepdims=True)
-        parts = [s[:, i * DH : (i + 1) * DH] for s in (t_sum, m_sum) for i in range(4)]
-        stats[place_in_order] = jnp.concatenate(parts, axis=0)
+            b = jnp.broadcast_to(jnp.concatenate([gb[j]] * (QN // DH), axis=1), (8, QN))
+            for i in range(SH // 16):
+                pair = []
+                for lo in (j * SH + i * 16, j * SH + i * 16 + 8):
+                    x = scores[lo : lo + 8] * scale - shift_in
+                    x = jnp.where(b + (lo - j * SH) <= query, jnp.maximum(x, 0.0), 0.0)
+                    w = jnp.exp2(jnp.log(x) * power)
+                    w_all[m, lo : lo + 8, :] = w
+                    pair.append(w * x)
+                    m_sum = m_sum + w
+                probs[lo - 8 : lo + 8, :] = jnp.concatenate(pair, axis=0).astype(BF16)
+        dv_acc[...] += dot(probs[...], gg[m])
+        stats[spot, 4:8, :] = lines(m_sum)
+
+    def match(m, spot):
+        dp = dot_nt(gv[...].reshape(KN, DH), gg[m])
+        dp_all[m] = dp
+        t_sum = jnp.zeros((8, QN), F32)
+        for lo in range(0, KN, 8):
+            t_sum = t_sum + w_all[m, lo : lo + 8, :] * dp[lo : lo + 8]
+        stats[spot, 0:4, :] = lines(t_sum)
 
     BATCH = ((0, 6), (6, 8))
 
@@ -226,44 +255,61 @@
             stats.at[lo:hi], stats_in.at[frm, lo:hi], s_send.at[batch, m], s_recv.at[batch, frm], row_of(yy, cc), c
         )
 
-    def pass_one(i, carry):
+    def spot_of(t, half):
+        yy = (y + 4 - place(t)) % 4
+        return yy * 2 + (core + half) % 2, 2 * t + half
+
+    def early(i):
+        return spot_of(i // 2 + i // 3, (i % 2) * (1 - i // 2))
+
+    def late(i):
+        return spot_of(i + 1 - i // 3, 1 - (i // 2) * (1 - i % 2))
+
+    def weigh_early(i, carry):
         @pl.when(i == 1)
         def _():
-            for kind, buf in both:
-                mate_copy(kind, buf, 0, False).wait_recv()
-
-        @pl.when(i == 3)
-        def _():
-            for kind, buf in both:
-                mate_copy(kind, buf, 1, False).wait_recv()
-
-        @pl.when(i == 4)
-        def _():
-            for kind, buf in both:
-                y_copy(kind, buf, 3, False).wait_recv()
-                mate_copy(kind, buf, 3, True).start()
-
-        @pl.when(i == 5)
-        def _():
-            for kind, buf in both:
-                mate_copy(kind, buf, 2, False).wait_recv()
-
-        @pl.when(i == 7)
-        def _():
-            for kind, buf in both:
-                mate_copy(kind, buf, 3, False).wait_recv()
-
-        yy = (y + 4 - place(i // 2)) % 4
-        first_pass(yy * 2 + (core + i) % 2, i)
-
-        @pl.when(i == 5)
+            from_mate(0)
+
+        for way in (0, 1):
+
+            @pl.when(i == 2 + way)
+            def _():
+                arrived(way, 1)
+
+        weigh(*early(i))
+        return carry
+
+    lax.fori_loop(0, 4, weigh_early, 0)
+    for j in far_first:
+        col_copy(1, j, False).wait_recv()
+
+    def match_early(i, carry):
+        match(*early(i))
+        return carry
+
+    lax.fori_loop(0, 4, match_early, 0)
+    for way in (0, 1):
+        arrived(way, 2)
+
+    def both_late(i, carry):
+        for step, t in ((0, 1), (1, 2), (3, 3)):
+
+            @pl.when(i == step)
+            def _():
+                from_mate(t)
+
+        m, spot = late(i)
+        weigh(m, spot)
+        match(m, spot)
+
+        @pl.when(i == 1)
         def _():
             for j in range(1, M):
                 stats_copy(0, j, True).start()
 
         return carry
 
-    lax.fori_loop(0, M, pass_one, 0)
+    lax.fori_loop(0, 4, both_late, 0)
     for j in range(1, M):
         stats_copy(1, j, True).start()
 
@@ -322,10 +368,10 @@
 
     def second_pass(m):
         row_shift = shifts[m]
-        for j in range(KN // 8):
-            lo = j * 8
-            probs[lo : lo + 8, :] = w_all[m, lo : lo + 8, :] * (dp_all[m, lo : lo + 8, :] - row_shift)
-        ds = probs[...].astype(BF16)
+        for lo in range(0, KN, 16):
+            pair = [w_all[m, i : i + 8, :] * (dp_all[m, i : i + 8, :] - row_shift) for i in (lo, lo + 8)]
+            probs[lo : lo + 16, :] = jnp.concatenate(pair, axis=0).astype(BF16)
+        ds = probs[...]
         dk_acc[...] += dot(ds, gq[m])
         return dot(kt[...], ds)
 
@@ -382,11 +428,13 @@
     dq_out[...] = (dq * FACTOR).astype(BF16)
     finish(0, dk_out, FACTOR)
 
-    for kind, buf in both:
-        for t in (1, 2, 3):
-            y_copy(kind, buf, t, True).wait_send()
+    for kind in (0, 1):
+        for way in (0, 1):
+            for stage in (0, 1, 2):
+                y_copy(kind, way, stage, True).wait_send()
         for t in range(4):
-            mate_copy(kind, buf, t, True).wait_send()
+            for part in (0, 1):
+                mate_copy(kind, t, part, True).wait_send()
     for kind in (0, 1, 2):
         for j in far_first:
             col_copy(kind, j, True).wait_send()
@@ -425,13 +473,13 @@
         out_specs=(vmem,) * 3,
         scratch_shapes=[
             S((N,), F32), S((4,), jnp.int32), S((2,), jnp.int32), V((N, QN), F32),
-            V((N, SH, DH), BF16), V((N, SH, DH), BF16), V((N, 8, DH), F32), V((8, DH), F32),
+            V((N, SH, DH), BF16), V((N, SH, DH), BF16), V((N, 1, DH), F32), V((1, DH), F32),
             V((M, QN, DH), BF16), V((M, QN, DH), BF16), V((M, 8, DH), F32),
-            V((DH, KN), BF16), V((M, KN, QN), F32), V((M, KN, QN), F32), V((KN, QN), F32),
+            V((DH, KN), BF16), V((M, KN, QN), F32), V((M, KN, QN), F32), V((KN, QN), BF16),
             V((KN, DH), F32), V((KN, DH), F32), V((M, 8, DH), F32), V((M, M, 8, DH), F32), V((M, 8, QN), F32),
             V((4, DH, QN), F32), V((4, DH, QN), BF16), V((4, DH, QN), BF16), V((4, DH, QN), BF16), V((3, DH, QN), BF16),
             V((N, SH, DH), BF16), V((N, SH, DH), BF16), V((N, SH, DH), BF16), V((N, SH, DH), BF16),
-            dma((8,)), dma((3, N)), dma((3, N)), dma((2, 3)), dma((2, 3)), dma((2, 4)), dma((2, 4)),
+            dma((8,)), dma((3, N)), dma((3, N)), dma((2, 2, 3)), dma((2, 2, 3)), dma((2, 4, 2)), dma((2, 4, 2)),
             dma((M,)), dma((M,)), dma((2, M)), dma((2, M)),
             dma((4,)), dma((4,)), dma((3,)), dma((3,)), dma((2, N)), dma((2, N)),
         ],

time: 54.7 us -> 49.8 us (0.910)
  Pallas kernels: 51.7 us -> 47.1 us
    pallas_call x1, Pallas kernels: 51.7 us -> 47.1 us  [local(): pl.pallas_call(kernel, out_shape=(jax.ShapeDtypeStruct((DH, QN), BF16), j...]
where the time goes in v3:
time: 49.8 us; the launch traced here: 49.7 us
  Pallas kernels  47.1 us (95%)
  local copies, waits for them, and re-layouts  1.92 us (4%)
  between operations  0.64 us (1%)
    pallas_call x1, Pallas kernels, local(): pl.pallas_call(kernel, out_shape=(jax.ShapeDtypeStruct((DH, QN), BF16), j...  47.1 us
    unnamed x3, local copies, waits for them, and re-layouts  1.92 us

profile of v3, /device:TPU:1, one launch (start us, length us, event | category | flops | bytes accessed | tf_op | source)
XLA Modules:
  0.0 49.7 jit_solution(9948924405419448042)
XLA Ops:
  0.6 47.1 %shard_map.103 = (bf16[128,512]{1,0:T(8,128)(2,1)S(1)}, bf16[128,256]{1,0:T(8,128)(2,1)S(1)}, bf16[128,256]{1,0:T(8,128)(2,1)S(1)}) custom-call(bf16[512,2048]{1,0:T(8,128)(2,1)} %queries.1, bf16[256,2048]{1,0:T(8,128)(2,1)} %keys.1, bf16[256,2048]{1,0:T(8,128)(2,1)} %values.1, bf16[512,2048]{1,0:T(8,128)(2,1)} %out_grad.1, f32[16,512]{1,0:T(8,128)} %tau_in.1, ...), custom_call_target="tpu_custom_call" | custom-call | tf_op jit(solution)/shard_map/pallas_call | solution.py:465
  47.7 0.7 %copy.14 = bf16[128,512]{1,0:T(8,128)(2,1)} copy(bf16[128,512]{1,0:T(8,128)(2,1)S(1)} %get-tuple-element.6) | data formatting | bytes 262144
  48.4 0.6 %copy.15 = bf16[128,256]{1,0:T(8,128)(2,1)} copy(bf16[128,256]{1,0:T(8,128)(2,1)S(1)} %get-tuple-element.7) | data formatting | bytes 131072
  49.0 0.6 %copy.16 = bf16[128,256]{1,0:T(8,128)(2,1)} copy(bf16[128,256]{1,0:T(8,128)(2,1)S(1)} %get-tuple-element.8) | data formatting | bytes 131072

commit v4 on v0

v4 whole, which is shorter than its diff:
```python
import math

import jax
import jax.numpy as jnp
from jax import lax
from jax.experimental import pallas as pl
from jax.experimental.pallas import tpu as pltpu
from jax.sharding import PartitionSpec as P

MESH = pl.DeviceIdType.MESH
DH = 128
BLK = 128
QN = 512
N = 16
SH = 32
KN = N * SH
Y = 4
F32 = jnp.float32
BF16 = jnp.bfloat16
FACTOR = 1.0 / math.sqrt(DH)


def dot(a, b):
    return jnp.dot(a, b, preferred_element_type=F32)


def dot_nt(a, b):
    return lax.dot_general(a, b, (((1,), (1,)), ((), ())), preferred_element_type=F32)


def place(t):
    return t + t // 2 - 2 * (t // 3)


def kernel(
    queries, keys, values, out_grad, tau_in, alpha_in, query_blocks_in, key_blocks_in,
    dq_out, dk_out, dv_out,
    alpha, query_blocks, key_blocks, tau,
    gk, gv, gb, gb_send,
    gq, gg, info,
    kt, w_all, dp_all, probs, dscore, dv_acc, dk_acc, dq_acc, stats, stats_in, shifts,
    core_out, core_in, dq_send, dq_in, own_part, row_part,
    in_sem, a_send, a_recv, x_send, x_recv, y_send, y_recv, i_send, i_recv, s_send, s_recv,
    c_send, c_recv, d_send, d_recv, p_send, p_recv,
):
    r = lax.axis_index("row")
    c = lax.axis_index("col")
    y = r // 4
    xh = (r // 2) % 2
    core = r % 2
    other = 1 - core
    share = y * 2 + core

    def row_of(yy, cc):
        return yy * 4 + xh * 2 + cc

    mate = row_of(y, other)

    def send(src, dst, ssem, rsem, row, col):
        return pltpu.make_async_remote_copy(
            src_ref=src, dst_ref=dst, send_sem=ssem, recv_sem=rsem,
            device_id=(row, col), device_id_type=MESH,
        )

    def landed(sem, ref):
        send(ref, ref, in_sem.at[0], sem, mate, c).wait_recv()

    def left(sem, ref):
        send(ref, ref, sem, in_sem.at[0], mate, c).wait_send()

    barrier = pltpu.get_barrier_semaphore()

    def greet(row, col):
        pl.semaphore_signal(barrier, inc=1, device_id=(row, col), device_id_type=MESH)

    for j in range(1, N):
        greet(r, (c + j) % N)
    for j in range(1, Y):
        greet(row_of((y + j) % Y, core), c)
    greet(mate, c)
    for j in range(1, N):
        greet((r + j) % N, r)

    @pl.when(c != r)
    def _():
        greet(r, r)

    key_rows = pl.ds(pl.multiple_of(share * SH, SH), SH)

    def head(h):
        return pl.ds(pl.multiple_of(h * DH, DH), DH)

    loads = [
        pltpu.make_async_copy(key_blocks_in, key_blocks, in_sem.at[0]),
        pltpu.make_async_copy(query_blocks_in, query_blocks, in_sem.at[1]),
        pltpu.make_async_copy(alpha_in, alpha, in_sem.at[2]),
        pltpu.make_async_copy(tau_in, tau, in_sem.at[3]),
        pltpu.make_async_copy(queries.at[:, head(c)], gq.at[y], in_sem.at[4]),
        pltpu.make_async_copy(out_grad.at[:, head(c)], gg.at[y], in_sem.at[5]),
        pltpu.make_async_copy(keys.at[key_rows, head(c)], gk.at[0, c], in_sem.at[6]),
        pltpu.make_async_copy(values.at[key_rows, head(c)], gv.at[0, c], in_sem.at[7]),
    ]
    for load in loads:
        load.start()
    apart = ((c + N - r) % N + N - 1) // N
    pl.semaphore_wait(barrier, (N - 1) + Y + (N - 1) + apart)

    far_first = sorted(range(1, N), key=lambda j: -min(j, N - j))

    def to_columns(kind):
        for j in far_first:
            peer = (c + j) % N
            src, dst = (
                (keys.at[key_rows, head(peer)], gk.at[0, c]),
                (values.at[key_rows, head(peer)], gv.at[0, c]),
                (gb_send, gb.at[c]),
            )[kind]
            send(src, dst, a_send.at[kind], a_recv.at[kind], r, peer).start()

    own = (queries, out_grad)
    group = (gq, gg)
    HALF = (pl.ds(0, QN // 2), pl.ds(QN // 2, QN // 2))

    def along_y(way, stage):
        step = 1 if way == 0 else 3
        part = HALF[way] if stage != 1 else HALF[1 - way]
        m = y if stage < 2 else (y + 4 - step) % Y
        for kind in (0, 1):
            dst = group[kind].at[m, part]
            src = own[kind].at[part, head(c)] if stage < 2 else dst
            send(
                src, dst, y_send.at[stage // 2], y_recv.at[way, stage], row_of((y + step) % Y, core), c
            ).start()

    def from_y(way, stage):
        landed(y_recv.at[way, stage], gq.at[0])

    to_columns(0)
    for way in (0, 1):
        along_y(way, 0)
    for load in loads[:4]:
        load.wait()
    base = (key_blocks[share // 4] * BLK + (share % 4) * SH).astype(F32)
    gb_send[...] = jnp.full((1, DH), base)
    gb[c] = gb_send[...]
    line = tau[pl.ds(c, 1), :]
    for i in range(4):
        info[y, i : i + 1, :] = line[:, i * DH : (i + 1) * DH]
        info[y, 4 + i : 5 + i, :] = jnp.full((1, DH), query_blocks[i] * BLK).astype(F32)
    to_columns(2)
    for j in range(1, Y):
        send(info.at[y], info.at[y], i_send, i_recv, row_of((y + j) % Y, core), c).start()
    to_columns(1)
    for way in (0, 1):
        along_y(way, 1)

    dk_acc[...] = jnp.zeros_like(dk_acc)
    excess = jnp.full((8, QN), alpha[c]) - 1.0
    scale = excess * FACTOR
    power = (1.0 - excess) / excess * (1.0 / math.log(2.0))
    lane = lax.broadcasted_iota(jnp.int32, (8, QN), 1) % BLK
    row8 = lax.broadcasted_iota(jnp.int32, (8, QN), 0)
    ahead = (lane - row8).astype(F32)

    def wide(tile, lo):
        line = jnp.concatenate([tile[lo + i : lo + i + 1, :] for i in range(4)], axis=1)
        return jnp.broadcast_to(line, (8, QN))

    for load in loads[4:]:
        load.wait()
    for way in (0, 1):
        from_y(way, 0)
        along_y(way, 2)
    landed(i_recv, info.at[0:3])
    landed(a_recv.at[0], gk.at[0, 0 : N - 1])
    to_mate_k = send(gk.at[0], gk.at[1], x_send.at[0], x_recv.at[0], mate, c)
    to_mate_v = send(gv.at[0], gv.at[1], x_send.at[1], x_recv.at[1], mate, c)
    to_mate_k.start()
    kt[0] = gk[0].reshape(KN, DH).T
    landed(a_recv.at[2], gb.at[0 : N - 1])

    def lines(total):
        total = jnp.sum(total, axis=0, keepdims=True)
        return jnp.concatenate([total[:, i * DH : (i + 1) * DH] for i in range(4)], axis=0)

    def member(t):
        return (y + 4 - place(t)) % Y

    def weigh(h, t):
        m = member(t)
        scores = dot_nt(gk[h].reshape(KN, DH), gq[m])
        tile = info[m]
        shift_in = wide(tile, 0) * excess
        query = wide(tile, 4) + ahead - (h * SH * (other - core)).astype(F32)
        m_sum = jnp.zeros((8, QN), F32)
        for j in range(N):
            b = jnp.broadcast_to(jnp.concatenate([gb[j]] * (QN // DH), axis=1), (8, QN))
            for i in range(SH // 16):
                pair = []
                for lo in (j * SH + i * 16, j * SH + i * 16 + 8):
                    x = scores[lo : lo + 8] * scale - shift_in
                    x = jnp.where(b + (lo - j * SH) <= query, jnp.maximum(x, 0.0), 0.0)
                    w = jnp.exp2(jnp.log(x) * power)
                    w_all[h, t, lo : lo + 8, :] = w
                    pair.append(w * x)
                    m_sum = m_sum + w
                probs[h, t, lo - 8 : lo + 8, :] = jnp.concatenate(pair, axis=0).astype(BF16)
        stats[h, t, 4:8, :] = lines(m_sum)

    def match(h, t):
        dp = dot_nt(gv[h].reshape(KN, DH), gg[member(t)])
        dp_all[h, t] = dp
        t_sum = jnp.zeros((8, QN), F32)
        for lo in range(0, KN, 8):
            t_sum = t_sum + w_all[h, t, lo : lo + 8, :] * dp[lo : lo + 8]
        stats[h, t, 0:4, :] = lines(t_sum)

    def sums_to_y(lo, hi):
        stats[0, lo:hi] = stats[0, lo:hi] + stats[1, lo:hi]
        for j in range(1, Y):
            send(
                stats.at[0, lo:hi], stats_in.at[y, lo:hi], s_send.at[lo // 3], s_recv.at[lo // 3],
                row_of((y + j) % Y, core), c,
            ).start()

    def weigh_early(i, carry):
        for way in (0, 1):

            @pl.when(i == 1 + way)
            def _():
                from_y(way, 1)

        @pl.when(i == 3)
        def _():
            landed(x_recv.at[0], gk.at[1])

        @pl.when(i == 4)
        def _():
            landed(a_recv.at[1], gv.at[0, 0 : N - 1])
            to_mate_v.start()

        weigh(i // 3, i % 3)
        return carry

    def match_early(i, carry):
        match(0, i)
        return carry

    def weigh_late(i, carry):
        weigh(i, 3)
        return carry

    def match_late(i, carry):
        @pl.when(i == 1)
        def _():
            landed(x_recv.at[1], gv.at[1])

        h = 1 - (4 - i) // 4
        match(h, 3 * (1 - h) + (i - 1) * h)

        @pl.when(i == 3)
        def _():
            sums_to_y(0, 3)

        return carry

    lax.fori_loop(0, 6, weigh_early, 0)
    lax.fori_loop(0, 3, match_early, 0)
    for way in (0, 1):
        from_y(way, 2)
    lax.fori_loop(0, 2, weigh_late, 0)
    lax.fori_loop(0, 5, match_late, 0)
    sums_to_y(3, 4)
    kt[1] = gk[1].reshape(KN, DH).T

    def core_copy(kind):
        return send(core_out.at[kind], core_in.at[kind], c_send.at[kind], c_recv.at[kind], mate, c)

    def add_values(i, carry):
        h = 1 - i // Y
        t = i % Y

        @pl.when(t == 0)
        def _():
            dv_acc[...] = jnp.zeros_like(dv_acc)

        dv_acc[...] += dot(probs[h, t], gg[member(t)])

        @pl.when(i == Y - 1)
        def _():
            core_out[1] = dv_acc[...].astype(BF16)
            core_copy(1).start()

        return carry

    lax.fori_loop(0, 2 * Y, add_values, 0)

    def send_last(kind, total):
        landed(c_recv.at[kind], core_in.at[kind])
        total = total + core_in[kind].astype(F32)
        own_part[kind] = total.astype(BF16).reshape(N, SH, DH)

        def one(j):
            peer = (c + j) % N
            send(
                own_part.at[kind, peer], row_part.at[kind, r], p_send.at[kind], p_recv.at[kind], c, peer
            ).start()

        for j in range(1, N):
            one(j)

        @pl.when(c != r)
        def _():
            one(0)

        @pl.when(c == r)
        def _():
            row_part[kind, r] = own_part[kind, c]

    def finish(kind, out, factor):
        @pl.when(c != r)
        def _():
            landed(p_recv.at[kind], row_part.at[kind])

        @pl.when(c == r)
        def _():
            landed(p_recv.at[kind], row_part.at[kind, 0 : N - 1])

        pairs = row_part[kind].astype(F32).reshape(4, 2, 2, SH, DH)
        pairs = (pairs[:, 0] + pairs[:, 1]).reshape(8 * SH, DH)
        out[...] = (pairs.T * factor).astype(BF16)

    landed(s_recv.at[0], stats_in.at[0:3, 0:3])
    landed(s_recv.at[1], stats_in.at[0:3, 3:4])
    stats_in[y] = stats[0]

    def one_shift(t, carry):
        m = member(t)
        total = jnp.zeros((8, DH), F32)
        for src in range(Y):
            total = total + stats_in[src, place((src + 4 - m) % Y)]
        shift = total[0:4] / jnp.maximum(total[4:8], 1.0)
        shifts[t] = wide(shift, 0)
        return carry

    lax.fori_loop(0, Y, one_shift, 0)

    def second_pass(h, t):
        row_shift = shifts[t]
        for lo in range(0, KN, 16):
            pair = [w_all[h, t, i : i + 8, :] * (dp_all[h, t, i : i + 8, :] - row_shift) for i in (lo, lo + 8)]
            dscore[lo : lo + 16, :] = jnp.concatenate(pair, axis=0).astype(BF16)
        ds = dscore[...]
        dk_acc[h] += dot(ds, gq[member(t)])
        return dot(kt[h], ds)

    def pass_two(i, carry):
        h = 1 - i // Y
        t = 3 - i % Y
        part = second_pass(h, t)

        @pl.when(h == 1)
        def _():
            dq_acc[t] = part

        @pl.when(i == Y - 1)
        def _():
            core_out[0] = dk_acc[1].astype(BF16)
            core_copy(0).start()

        @pl.when(h == 0)
        def _():
            dq_acc[t] += part
            dq_send[t] = dq_acc[t].astype(BF16)

        for tt in (3, 2, 1):

            @pl.when(i == 2 * Y - 1 - tt)
            def _():
                send(dq_send.at[tt], dq_in.at[tt - 1], d_send, d_recv, row_of(member(tt), core), c).start()

        @pl.when(i == 1)
        def _():
            send_last(1, dv_acc[...])

        return carry

    lax.fori_loop(0, 2 * Y, pass_two, 0)
    send_last(0, dk_acc[0])
    finish(1, dv_out, 1.0)
    landed(d_recv, dq_in)
    dq = dq_acc[0]
    for t in range(3):
        dq = dq + dq_in[t].astype(F32)
    dq_out[...] = (dq * FACTOR).astype(BF16)
    finish(0, dk_out, FACTOR)

    left(a_send.at[0], gk.at[0, 0 : N - 1])
    left(a_send.at[1], gv.at[0, 0 : N - 1])
    left(a_send.at[2], gb.at[0 : N - 1])
    left(i_send, info.at[0:3])
    left(y_send.at[0], gq)
    left(y_send.at[1], gq.at[0:2])
    to_mate_k.wait_send()
    to_mate_v.wait_send()
    left(s_send.at[0], stats_in.at[0:3, 0:3])
    left(s_send.at[1], stats_in.at[0:3, 3:4])
    left(d_send, dq_in)
    for kind in (0, 1):
        core_copy(kind).wait_send()

        @pl.when(c != r)
        def _():
            left(p_send.at[kind], own_part.at[kind])

        @pl.when(c == r)
        def _():
            left(p_send.at[kind], own_part.at[kind, 0 : N - 1])


def local(*args):
    hbm = pl.BlockSpec(memory_space=pltpu.HBM)
    vmem = pl.BlockSpec(memory_space=pltpu.VMEM)
    V = pltpu.VMEM
    S = pltpu.SMEM
    dma = pltpu.SemaphoreType.DMA
    one = pltpu.SemaphoreType.DMA(())
    return pl.pallas_call(
        kernel,
        out_shape=(
            jax.ShapeDtypeStruct((DH, QN), BF16),
            jax.ShapeDtypeStruct((DH, 2 * BLK), BF16),
            jax.ShapeDtypeStruct((DH, 2 * BLK), BF16),
        ),
        in_specs=[hbm] * 8,
        out_specs=(vmem,) * 3,
        scratch_shapes=[
            S((N,), F32), S((4,), jnp.int32), S((2,), jnp.int32), V((N, QN), F32),
            V((2, N, SH, DH), BF16), V((2, N, SH, DH), BF16), V((N, 1, DH), F32), V((1, DH), F32),
            V((Y, QN, DH), BF16), V((Y, QN, DH), BF16), V((Y, 8, DH), F32),
            V((2, DH, KN), BF16), V((2, Y, KN, QN), F32), V((2, Y, KN, QN), F32), V((2, Y, KN, QN), BF16), V((KN, QN), BF16),
            V((KN, DH), F32), V((2, KN, DH), F32), V((Y, DH, QN), F32), V((2, Y, 8, DH), F32), V((Y, Y, 8, DH), F32), V((Y, 8, QN), F32),
            V((2, KN, DH), BF16), V((2, KN, DH), BF16), V((Y, DH, QN), BF16), V((3, DH, QN), BF16),
            V((2, N, SH, DH), BF16), V((2, N, SH, DH), BF16),
            dma((8,)), dma((3,)), dma((3,)), dma((2,)), dma((2,)), dma((2,)), dma((2, 3)), one, one, dma((2,)), dma((2,)),
            dma((2,)), dma((2,)), one, one, dma((2,)), dma((2,)),
        ],
        compiler_params=pltpu.CompilerParams(
            collective_id=0, has_side_effects=True, vmem_limit_bytes=48 * 1024 * 1024
        ),
    )(*[pltpu.with_memory_space_constraint(a, pltpu.HBM) for a in args])


def solution(mesh):
    in_specs = (
        P("row", None), P("col", None), P("col", None), P("row", None),
        P(None, "row"), P(), P("row"), P("col"),
    )
    out_specs = (P("col", "row"), P("row", "col"), P("row", "col"))
    return jax.shard_map(local, mesh=mesh, in_specs=in_specs, out_specs=out_specs, check_vma=False)
```

time: 704 us -> 44.3 us (0.06); the launches traced: 696 us -> 44 us
  waiting for transfers between devices: 299 us -> 0 us
  matrix products: 134 us -> 0 us
  local copies, waits for them, and re-layouts: 124 us -> 1.92 us
  loops' own time: 108 us -> 0 us
  Pallas kernels: 0 us -> 41.5 us
  other arithmetic: 16.3 us -> 0 us
  between operations: 13.8 us -> 0.64 us
    reduce_scatter x2 -> x0, waiting for transfers between devices: 187 us -> none  [the longest x1 99.4 us: local(): lax.psum_scatter(factor * jnp.einsum('hqk,khd->hdq', score_grad, columns,...]
    dot_general x67 -> x0, matrix products: 134 us -> none  [the longest x32 77.2 us: head_parts(): jnp.einsum('qd,kd->qk', query_head, key_head, preferred_element_type=jnp....]
    psum x1 -> x0, waiting for transfers between devices: 112 us -> none  [local(): totals, masses = lax.psum((totals, masses), 'col')]
    another operation x2 -> x0, loops' own time: 108 us -> none  [the longest x1 55 us: local(): probabilities, totals, masses = lax.map(first_pass, head_ids)]
    dynamic_slice x96 -> x0, local copies, waits for them, and re-layouts: 72.8 us -> none  [the longest x32 29.8 us: head_parts(): excess = alpha[head] - 1.0]
    dynamic_update_slice x32 -> x0, local copies, waits for them, and re-layouts: 43 us -> none  [local(): probabilities, totals, masses = lax.map(first_pass, head_ids)]
    pallas_call x0 -> x1, Pallas kernels: none -> 41.5 us  [local(): pl.pallas_call(kernel, out_shape=(jax.ShapeDtypeStruct((DH, QN), BF16), j...]
    reduce_sum x16 -> x0, other arithmetic: 8.96 us -> none  [first_pass(): jnp.sum(weights_h, axis=1)]
  transfers between devices with their start and end apart: 3 -> 0, of which waited for: 3 -> 0; matrix products, arithmetic and copies ran while one was open for 3% -> 0% of each run, Pallas kernels for 0% -> 0%
where the time goes in v4:
time: 44.3 us; the launch traced here: 44 us
  Pallas kernels  41.5 us (94%)
  local copies, waits for them, and re-layouts  1.92 us (4%)
  between operations  0.64 us (1%)
    pallas_call x1, Pallas kernels, local(): pl.pallas_call(kernel, out_shape=(jax.ShapeDtypeStruct((DH, QN), BF16), j...  41.5 us
    unnamed x3, local copies, waits for them, and re-layouts  1.92 us

profile of v4, /device:TPU:1, one launch (start us, length us, event | category | flops | bytes accessed | tf_op | source)
XLA Modules:
  0.0 44.0 jit_solution(9743834792841999633)
XLA Ops:
  0.6 41.5 %shard_map.103 = (bf16[128,512]{1,0:T(8,128)(2,1)S(1)}, bf16[128,256]{1,0:T(8,128)(2,1)S(1)}, bf16[128,256]{1,0:T(8,128)(2,1)S(1)}) custom-call(bf16[512,2048]{1,0:T(8,128)(2,1)} %queries.1, bf16[256,2048]{1,0:T(8,128)(2,1)} %keys.1, bf16[256,2048]{1,0:T(8,128)(2,1)} %values.1, bf16[512,2048]{1,0:T(8,128)(2,1)} %out_grad.1, f32[16,512]{1,0:T(8,128)} %tau_in.1, ...), custom_call_target="tpu_custom_call" | custom-call | tf_op jit(solution)/shard_map/pallas_call | solution.py:428
  42.1 0.7 %copy.14 = bf16[128,512]{1,0:T(8,128)(2,1)} copy(bf16[128,512]{1,0:T(8,128)(2,1)S(1)} %get-tuple-element.6) | data formatting | bytes 262144
  42.7 0.6 %copy.15 = bf16[128,256]{1,0:T(8,128)(2,1)} copy(bf16[128,256]{1,0:T(8,128)(2,1)S(1)} %get-tuple-element.7) | data formatting | bytes 131072
  43.4 0.6 %copy.16 = bf16[128,256]{1,0:T(8,128)(2,1)} copy(bf16[128,256]{1,0:T(8,128)(2,1)S(1)} %get-tuple-element.8) | data formatting | bytes 131072

commit v5 on v4

--- a/solution.py
+++ b/solution.py
@@ -38,10 +38,10 @@
     alpha, query_blocks, key_blocks, tau,
     gk, gv, gb, gb_send,
     gq, gg, info,
-    kt, w_all, dp_all, probs, dscore, dv_acc, dk_acc, dq_acc, stats, stats_in, shifts,
+    kt, w_all, dp_all, probs, dv_acc, dk_acc, dq_own, stats, stats_in, shifts,
     core_out, core_in, dq_send, dq_in, own_part, row_part,
     in_sem, a_send, a_recv, x_send, x_recv, y_send, y_recv, i_send, i_recv, s_send, s_recv,
-    c_send, c_recv, d_send, d_recv, p_send, p_recv,
+    c_send, c_recv, d_send, d_recv, p_send, p_recv, ready,
 ):
     r = lax.axis_index("row")
     c = lax.axis_index("col")
@@ -73,17 +73,14 @@
     def greet(row, col):
         pl.semaphore_signal(barrier, inc=1, device_id=(row, col), device_id_type=MESH)
 
-    for j in range(1, N):
+    far_first = sorted(range(1, N), key=lambda j: -min(j, N - j))
+    across = y * 4 + (1 - xh) * 2 + core
+    for j in far_first:
         greet(r, (c + j) % N)
+    greet(across, c)
     for j in range(1, Y):
         greet(row_of((y + j) % Y, core), c)
     greet(mate, c)
-    for j in range(1, N):
-        greet((r + j) % N, r)
-
-    @pl.when(c != r)
-    def _():
-        greet(r, r)
 
     key_rows = pl.ds(pl.multiple_of(share * SH, SH), SH)
 
@@ -102,10 +99,8 @@
     ]
     for load in loads:
         load.start()
-    apart = ((c + N - r) % N + N - 1) // N
-    pl.semaphore_wait(barrier, (N - 1) + Y + (N - 1) + apart)
-
-    far_first = sorted(range(1, N), key=lambda j: -min(j, N - j))
+    pl.semaphore_wait(barrier, N + Y)
+    pl.semaphore_signal(ready, inc=1, device_id=(across, c), device_id_type=MESH)
 
     def to_columns(kind):
         for j in far_first:
@@ -175,6 +170,7 @@
     landed(a_recv.at[0], gk.at[0, 0 : N - 1])
     to_mate_k = send(gk.at[0], gk.at[1], x_send.at[0], x_recv.at[0], mate, c)
     to_mate_v = send(gv.at[0], gv.at[1], x_send.at[1], x_recv.at[1], mate, c)
+    pl.semaphore_wait(ready, 1)
     to_mate_k.start()
     kt[0] = gk[0].reshape(KN, DH).T
     landed(a_recv.at[2], gb.at[0 : N - 1])
@@ -223,6 +219,32 @@
                 row_of((y + j) % Y, core), c,
             ).start()
 
+    def weigh_and_match(h, t):
+        m = member(t)
+        scores = dot_nt(gk[h].reshape(KN, DH), gq[m])
+        dp = dot_nt(gv[h].reshape(KN, DH), gg[m])
+        dp_all[h, t] = dp
+        tile = info[m]
+        shift_in = wide(tile, 0) * excess
+        query = wide(tile, 4) + ahead - (h * SH * (other - core)).astype(F32)
+        t_sum = jnp.zeros((8, QN), F32)
+        m_sum = jnp.zeros((8, QN), F32)
+        for j in range(N):
+            b = jnp.broadcast_to(jnp.concatenate([gb[j]] * (QN // DH), axis=1), (8, QN))
+            for i in range(SH // 16):
+                pair = []
+                for lo in (j * SH + i * 16, j * SH + i * 16 + 8):
+                    x = scores[lo : lo + 8] * scale - shift_in
+                    x = jnp.where(b + (lo - j * SH) <= query, jnp.maximum(x, 0.0), 0.0)
+                    w = jnp.exp2(jnp.log(x) * power)
+                    w_all[h, t, lo : lo + 8, :] = w
+                    pair.append(w * x)
+                    t_sum = t_sum + w * dp[lo : lo + 8]
+                    m_sum = m_sum + w
+                probs[h, t, lo - 8 : lo + 8, :] = jnp.concatenate(pair, axis=0).astype(BF16)
+        stats[h, t, 0:4, :] = lines(t_sum)
+        stats[h, t, 4:8, :] = lines(m_sum)
+
     def weigh_early(i, carry):
         for way in (0, 1):
 
@@ -242,34 +264,33 @@
         weigh(i // 3, i % 3)
         return carry
 
-    def match_early(i, carry):
+    def match_own(i, carry):
         match(0, i)
         return carry
 
-    def weigh_late(i, carry):
-        weigh(i, 3)
-        return carry
-
-    def match_late(i, carry):
+    def match_other(i, carry):
+        match(1, i)
+        return carry
+
+    def rest(i, carry):
         @pl.when(i == 1)
         def _():
             landed(x_recv.at[1], gv.at[1])
-
-        h = 1 - (4 - i) // 4
-        match(h, 3 * (1 - h) + (i - 1) * h)
-
-        @pl.when(i == 3)
+            lax.fori_loop(0, 2, match_other, 0)
+
+        weigh_and_match(1 - (2 - i) // 2, 3 - i % 2)
+
+        @pl.when(i == 1)
         def _():
             sums_to_y(0, 3)
 
         return carry
 
-    lax.fori_loop(0, 6, weigh_early, 0)
-    lax.fori_loop(0, 3, match_early, 0)
+    lax.fori_loop(0, 5, weigh_early, 0)
+    lax.fori_loop(0, 3, match_own, 0)
     for way in (0, 1):
         from_y(way, 2)
-    lax.fori_loop(0, 2, weigh_late, 0)
-    lax.fori_loop(0, 5, match_late, 0)
+    lax.fori_loop(0, 3, rest, 0)
     sums_to_y(3, 4)
     kt[1] = gk[1].reshape(KN, DH).T
 
@@ -293,7 +314,7 @@
 
         return carry
 
-    lax.fori_loop(0, 2 * Y, add_values, 0)
+    lax.fori_loop(0, 2 * Y, add_values, 0, unroll=2)
 
     def send_last(kind, total):
         landed(c_recv.at[kind], core_in.at[kind])
@@ -345,51 +366,52 @@
 
     lax.fori_loop(0, Y, one_shift, 0)
 
-    def second_pass(h, t):
+    def score_grad(h, t):
         row_shift = shifts[t]
         for lo in range(0, KN, 16):
             pair = [w_all[h, t, i : i + 8, :] * (dp_all[h, t, i : i + 8, :] - row_shift) for i in (lo, lo + 8)]
-            dscore[lo : lo + 16, :] = jnp.concatenate(pair, axis=0).astype(BF16)
-        ds = dscore[...]
+            probs[h, t, lo : lo + 16, :] = jnp.concatenate(pair, axis=0).astype(BF16)
+        ds = probs[h, t]
         dk_acc[h] += dot(ds, gq[member(t)])
-        return dot(kt[h], ds)
-
-    def pass_two(i, carry):
-        h = 1 - i // Y
-        t = 3 - i % Y
-        part = second_pass(h, t)
-
-        @pl.when(h == 1)
-        def _():
-            dq_acc[t] = part
-
-        @pl.when(i == Y - 1)
-        def _():
-            core_out[0] = dk_acc[1].astype(BF16)
-            core_copy(0).start()
-
-        @pl.when(h == 0)
-        def _():
-            dq_acc[t] += part
-            dq_send[t] = dq_acc[t].astype(BF16)
+        return ds
+
+    def other_share(i, carry):
+        score_grad(1, 3 - i)
+        return carry
+
+    def own_share(i, carry):
+        t = 3 - i
+        ds = score_grad(0, t)
+        part = dot(kt[0], ds) + dot(kt[1], probs[1, t])
+
+        @pl.when(t == 0)
+        def _():
+            dq_own[...] = part
+
+        @pl.when(t > 0)
+        def _():
+            dq_send[t] = part.astype(BF16)
 
         for tt in (3, 2, 1):
 
-            @pl.when(i == 2 * Y - 1 - tt)
+            @pl.when(t == tt)
             def _():
                 send(dq_send.at[tt], dq_in.at[tt - 1], d_send, d_recv, row_of(member(tt), core), c).start()
 
-        @pl.when(i == 1)
+        @pl.when(i == 0)
         def _():
             send_last(1, dv_acc[...])
 
         return carry
 
-    lax.fori_loop(0, 2 * Y, pass_two, 0)
+    lax.fori_loop(0, Y, other_share, 0, unroll=2)
+    core_out[0] = dk_acc[1].astype(BF16)
+    core_copy(0).start()
+    lax.fori_loop(0, Y, own_share, 0, unroll=2)
     send_last(0, dk_acc[0])
     finish(1, dv_out, 1.0)
     landed(d_recv, dq_in)
-    dq = dq_acc[0]
+    dq = dq_own[...]
     for t in range(3):
         dq = dq + dq_in[t].astype(F32)
     dq_out[...] = (dq * FACTOR).astype(BF16)
@@ -438,12 +460,12 @@
             S((N,), F32), S((4,), jnp.int32), S((2,), jnp.int32), V((N, QN), F32),
             V((2, N, SH, DH), BF16), V((2, N, SH, DH), BF16), V((N, 1, DH), F32), V((1, DH), F32),
             V((Y, QN, DH), BF16), V((Y, QN, DH), BF16), V((Y, 8, DH), F32),
-            V((2, DH, KN), BF16), V((2, Y, KN, QN), F32), V((2, Y, KN, QN), F32), V((2, Y, KN, QN), BF16), V((KN, QN), BF16),
-            V((KN, DH), F32), V((2, KN, DH), F32), V((Y, DH, QN), F32), V((2, Y, 8, DH), F32), V((Y, Y, 8, DH), F32), V((Y, 8, QN), F32),
+            V((2, DH, KN), BF16), V((2, Y, KN, QN), F32), V((2, Y, KN, QN), F32), V((2, Y, KN, QN), BF16),
+            V((KN, DH), F32), V((2, KN, DH), F32), V((DH, QN), F32), V((2, Y, 8, DH), F32), V((Y, Y, 8, DH), F32), V((Y, 8, QN), F32),
             V((2, KN, DH), BF16), V((2, KN, DH), BF16), V((Y, DH, QN), BF16), V((3, DH, QN), BF16),
             V((2, N, SH, DH), BF16), V((2, N, SH, DH), BF16),
             dma((8,)), dma((3,)), dma((3,)), dma((2,)), dma((2,)), dma((2,)), dma((2, 3)), one, one, dma((2,)), dma((2,)),
-            dma((2,)), dma((2,)), one, one, dma((2,)), dma((2,)),
+            dma((2,)), dma((2,)), one, one, dma((2,)), dma((2,)), pltpu.SemaphoreType.REGULAR,
         ],
         compiler_params=pltpu.CompilerParams(
             collective_id=0, has_side_effects=True, vmem_limit_bytes=48 * 1024 * 1024

time: 44.3 us -> 43.2 us (0.975)
  Pallas kernels: 41.5 us -> 40.6 us
    pallas_call x1, Pallas kernels: 41.5 us -> 40.6 us  [local(): pl.pallas_call(kernel, out_shape=(jax.ShapeDtypeStruct((DH, QN), BF16), j...]
where the time goes in v5:
time: 43.2 us
  Pallas kernels  40.6 us (94%)
  local copies, waits for them, and re-layouts  1.92 us (4%)
  between operations  0.64 us (1%)
    pallas_call x1, Pallas kernels, local(): pl.pallas_call(kernel, out_shape=(jax.ShapeDtypeStruct((DH, QN), BF16), j...  40.6 us
    unnamed x3, local copies, waits for them, and re-layouts  1.92 us

profile of v5, /device:TPU:1, one launch (start us, length us, event | category | flops | bytes accessed | tf_op | source)
XLA Modules:
  0.0 43.2 jit_solution(9801311976287718337)
XLA Ops:
  0.6 40.6 %shard_map.103 = (bf16[128,512]{1,0:T(8,128)(2,1)S(1)}, bf16[128,256]{1,0:T(8,128)(2,1)S(1)}, bf16[128,256]{1,0:T(8,128)(2,1)S(1)}) custom-call(bf16[512,2048]{1,0:T(8,128)(2,1)} %queries.1, bf16[256,2048]{1,0:T(8,128)(2,1)} %keys.1, bf16[256,2048]{1,0:T(8,128)(2,1)} %values.1, bf16[512,2048]{1,0:T(8,128)(2,1)} %out_grad.1, f32[16,512]{1,0:T(8,128)} %tau_in.1, ...), custom_call_target="tpu_custom_call" | custom-call | tf_op jit(solution)/shard_map/pallas_call | solution.py:450
  41.2 0.7 %copy.14 = bf16[128,512]{1,0:T(8,128)(2,1)} copy(bf16[128,512]{1,0:T(8,128)(2,1)S(1)} %get-tuple-element.6) | data formatting | bytes 262144
  41.9 0.6 %copy.15 = bf16[128,256]{1,0:T(8,128)(2,1)} copy(bf16[128,256]{1,0:T(8,128)(2,1)S(1)} %get-tuple-element.7) | data formatting | bytes 131072
  42.5 0.6 %copy.16 = bf16[128,256]{1,0:T(8,128)(2,1)} copy(bf16[128,256]{1,0:T(8,128)(2,1)S(1)} %get-tuple-element.8) | data formatting | bytes 131072

commit v6 on v5

--- a/solution.py
+++ b/solution.py
@@ -440,6 +440,17 @@
             left(p_send.at[kind], own_part.at[kind, 0 : N - 1])
 
 
+def store(dq, dk, dv, dq_out, dk_out, dv_out, sem):
+    copies = [
+        pltpu.make_async_copy(src, dst, sem.at[i])
+        for i, (src, dst) in enumerate(((dq, dq_out), (dk, dk_out), (dv, dv_out)))
+    ]
+    for copy in copies:
+        copy.start()
+    for copy in copies:
+        copy.wait()
+
+
 def local(*args):
     hbm = pl.BlockSpec(memory_space=pltpu.HBM)
     vmem = pl.BlockSpec(memory_space=pltpu.VMEM)
@@ -447,13 +458,14 @@
     S = pltpu.SMEM
     dma = pltpu.SemaphoreType.DMA
     one = pltpu.SemaphoreType.DMA(())
-    return pl.pallas_call(
+    shapes = (
+        jax.ShapeDtypeStruct((DH, QN), BF16),
+        jax.ShapeDtypeStruct((DH, 2 * BLK), BF16),
+        jax.ShapeDtypeStruct((DH, 2 * BLK), BF16),
+    )
+    grads = pl.pallas_call(
         kernel,
-        out_shape=(
-            jax.ShapeDtypeStruct((DH, QN), BF16),
-            jax.ShapeDtypeStruct((DH, 2 * BLK), BF16),
-            jax.ShapeDtypeStruct((DH, 2 * BLK), BF16),
-        ),
+        out_shape=shapes,
         in_specs=[hbm] * 8,
         out_specs=(vmem,) * 3,
         scratch_shapes=[
@@ -472,6 +484,13 @@
         ),
     )(*[pltpu.with_memory_space_constraint(a, pltpu.HBM) for a in args])
 
+    return pl.pallas_call(
+        store,
+        out_shape=shapes,
+        in_specs=[vmem] * 3,
+        out_specs=(hbm,) * 3,
+        scratch_shapes=[dma((3,))],
+    )(*[pltpu.with_memory_space_constraint(g, pltpu.VMEM) for g in grads])
 
 def solution(mesh):
     in_specs = (

time: 43.2 us -> 42.1 us (0.975)
  local copies, waits for them, and re-layouts: 1.92 us -> 0 us
  Pallas kernels: 40.6 us -> 41.3 us
    unnamed x3 -> x0, local copies, waits for them, and re-layouts: 1.92 us -> none
    pallas_call x1 -> x2, Pallas kernels: 40.6 us -> 41.3 us  [the longest x1 40.6 us: local(): pl.pallas_call(kernel, out_shape=shapes, in_specs=[hbm] * 8, out_specs=(v...]
where the time goes in v6:
time: 42.1 us; the launch traced here: 42 us
  Pallas kernels  41.3 us (98%)
  between operations  0.64 us (2%)
    pallas_call x1, Pallas kernels, local(): pl.pallas_call(kernel, out_shape=shapes, in_specs=[hbm] * 8, out_specs=(v...  40.6 us

profile of v6, /device:TPU:1, one launch (start us, length us, event | category | flops | bytes accessed | tf_op | source)
XLA Modules:
  0.0 42.0 jit_solution(5160093426556413662)
XLA Ops:
  0.6 40.6 %shard_map.103 = (bf16[128,512]{1,0:T(8,128)(2,1)S(1)}, bf16[128,256]{1,0:T(8,128)(2,1)S(1)}, bf16[128,256]{1,0:T(8,128)(2,1)S(1)}) custom-call(bf16[512,2048]{1,0:T(8,128)(2,1)} %queries.1, bf16[256,2048]{1,0:T(8,128)(2,1)} %keys.1, bf16[256,2048]{1,0:T(8,128)(2,1)} %values.1, bf16[512,2048]{1,0:T(8,128)(2,1)} %out_grad.1, f32[16,512]{1,0:T(8,128)} %tau_in.1, ...), custom_call_target="tpu_custom_call" | custom-call | tf_op jit(solution)/shard_map/pallas_call | solution.py:466
  41.2 0.7 %shard_map.104 = (bf16[128,512]{1,0:T(8,128)(2,1)}, bf16[128,256]{1,0:T(8,128)(2,1)}, bf16[128,256]{1,0:T(8,128)(2,1)}) custom-call(bf16[128,512]{1,0:T(8,128)(2,1)S(1)} %get-tuple-element.6.dq, bf16[128,256]{1,0:T(8,128)(2,1)S(1)} %get-tuple-element.7.dk, bf16[128,256]{1,0:T(8,128)(2,1)S(1)} %get-tuple-element.8.dv), custom_call_target="tpu_custom_call" | custom-call | tf_op jit(solution)/shard_map/pallas_call | solution.py:487

commit v7 on v6

--- a/solution.py
+++ b/solution.py
@@ -327,7 +327,7 @@
                 own_part.at[kind, peer], row_part.at[kind, r], p_send.at[kind], p_recv.at[kind], c, peer
             ).start()
 
-        for j in range(1, N):
+        for j in far_first:
             one(j)
 
         @pl.when(c != r)
@@ -398,7 +398,7 @@
             def _():
                 send(dq_send.at[tt], dq_in.at[tt - 1], d_send, d_recv, row_of(member(tt), core), c).start()
 
-        @pl.when(i == 0)
+        @pl.when(i == 1)
         def _():
             send_last(1, dv_acc[...])
 

time: 42.1 us -> 41.8 us (level)
  Pallas kernels: 41.3 us -> 40.6 us
    pallas_call x1, Pallas kernels: 40.6 us -> 39.9 us  [local(): pl.pallas_call(kernel, out_shape=shapes, in_specs=[hbm] * 8, out_specs=(v...]
where the time goes in v7:
time: 41.8 us; the launch traced here: 41.3 us
  Pallas kernels  40.6 us (97%)
  between operations  0.64 us (2%)
    pallas_call x1, Pallas kernels, local(): pl.pallas_call(kernel, out_shape=shapes, in_specs=[hbm] * 8, out_specs=(v...  39.9 us

profile of v7, /device:TPU:1, one launch (start us, length us, event | category | flops | bytes accessed | tf_op | source)
XLA Modules:
  0.0 41.3 jit_solution(11851175098088457594)
XLA Ops:
  0.6 39.9 %shard_map.103 = (bf16[128,512]{1,0:T(8,128)(2,1)S(1)}, bf16[128,256]{1,0:T(8,128)(2,1)S(1)}, bf16[128,256]{1,0:T(8,128)(2,1)S(1)}) custom-call(bf16[512,2048]{1,0:T(8,128)(2,1)} %queries.1, bf16[256,2048]{1,0:T(8,128)(2,1)} %keys.1, bf16[256,2048]{1,0:T(8,128)(2,1)} %values.1, bf16[512,2048]{1,0:T(8,128)(2,1)} %out_grad.1, f32[16,512]{1,0:T(8,128)} %tau_in.1, ...), custom_call_target="tpu_custom_call" | custom-call | tf_op jit(solution)/shard_map/pallas_call | solution.py:466
  40.6 0.7 %shard_map.104 = (bf16[128,512]{1,0:T(8,128)(2,1)}, bf16[128,256]{1,0:T(8,128)(2,1)}, bf16[128,256]{1,0:T(8,128)(2,1)}) custom-call(bf16[128,512]{1,0:T(8,128)(2,1)S(1)} %get-tuple-element.6.dq, bf16[128,256]{1,0:T(8,128)(2,1)S(1)} %get-tuple-element.7.dk, bf16[128,256]{1,0:T(8,128)(2,1)S(1)} %get-tuple-element.8.dv), custom_call_target="tpu_custom_call" | custom-call | tf_op jit(solution)/shard_map/pallas_call | solution.py:487

commit v8 on v7

--- a/solution.py
+++ b/solution.py
@@ -38,7 +38,7 @@
     alpha, query_blocks, key_blocks, tau,
     gk, gv, gb, gb_send,
     gq, gg, info,
-    kt, w_all, dp_all, probs, dv_acc, dk_acc, dq_own, stats, stats_in, shifts,
+    kt, w_all, dp_all, probs, dv_acc, dk_acc, stats, stats_in, shifts,
     core_out, core_in, dq_send, dq_in, own_part, row_part,
     in_sem, a_send, a_recv, x_send, x_recv, y_send, y_recv, i_send, i_recv, s_send, s_recv,
     c_send, c_recv, d_send, d_recv, p_send, p_recv, ready,
@@ -382,15 +382,9 @@
     def own_share(i, carry):
         t = 3 - i
         ds = score_grad(0, t)
-        part = dot(kt[0], ds) + dot(kt[1], probs[1, t])
-
-        @pl.when(t == 0)
-        def _():
-            dq_own[...] = part
-
         @pl.when(t > 0)
         def _():
-            dq_send[t] = part.astype(BF16)
+            dq_send[t] = (dot(kt[0], ds) + dot(kt[1], probs[1, t])).astype(BF16)
 
         for tt in (3, 2, 1):
 
@@ -409,9 +403,9 @@
     core_copy(0).start()
     lax.fori_loop(0, Y, own_share, 0, unroll=2)
     send_last(0, dk_acc[0])
+    dq = dot(kt[0], probs[0, 0]) + dot(kt[1], probs[1, 0])
     finish(1, dv_out, 1.0)
     landed(d_recv, dq_in)
-    dq = dq_own[...]
     for t in range(3):
         dq = dq + dq_in[t].astype(F32)
     dq_out[...] = (dq * FACTOR).astype(BF16)
@@ -473,7 +467,7 @@
             V((2, N, SH, DH), BF16), V((2, N, SH, DH), BF16), V((N, 1, DH), F32), V((1, DH), F32),
             V((Y, QN, DH), BF16), V((Y, QN, DH), BF16), V((Y, 8, DH), F32),
             V((2, DH, KN), BF16), V((2, Y, KN, QN), F32), V((2, Y, KN, QN), F32), V((2, Y, KN, QN), BF16),
-            V((KN, DH), F32), V((2, KN, DH), F32), V((DH, QN), F32), V((2, Y, 8, DH), F32), V((Y, Y, 8, DH), F32), V((Y, 8, QN), F32),
+            V((KN, DH), F32), V((2, KN, DH), F32), V((2, Y, 8, DH), F32), V((Y, Y, 8, DH), F32), V((Y, 8, QN), F32),
             V((2, KN, DH), BF16), V((2, KN, DH), BF16), V((Y, DH, QN), BF16), V((3, DH, QN), BF16),
             V((2, N, SH, DH), BF16), V((2, N, SH, DH), BF16),
             dma((8,)), dma((3,)), dma((3,)), dma((2,)), dma((2,)), dma((2,)), dma((2, 3)), one, one, dma((2,)), dma((2,)),

time: 41.8 us -> 41.6 us (level)
  no operation moved by 1% of the time
where the time goes in v8:
time: 41.6 us; the launch traced here: 41.3 us
  Pallas kernels  40.7 us (98%)
  between operations  0.64 us (2%)
    pallas_call x1, Pallas kernels, local(): pl.pallas_call(kernel, out_shape=shapes, in_specs=[hbm] * 8, out_specs=(v...  40 us

profile of v8, /device:TPU:1, one launch (start us, length us, event | category | flops | bytes accessed | tf_op | source)
XLA Modules:
  0.0 41.3 jit_solution(15531058054799976371)
XLA Ops:
  0.6 40.0 %shard_map.103 = (bf16[128,512]{1,0:T(8,128)(2,1)S(1)}, bf16[128,256]{1,0:T(8,128)(2,1)S(1)}, bf16[128,256]{1,0:T(8,128)(2,1)S(1)}) custom-call(bf16[512,2048]{1,0:T(8,128)(2,1)} %queries.1, bf16[256,2048]{1,0:T(8,128)(2,1)} %keys.1, bf16[256,2048]{1,0:T(8,128)(2,1)} %values.1, bf16[512,2048]{1,0:T(8,128)(2,1)} %out_grad.1, f32[16,512]{1,0:T(8,128)} %tau_in.1, ...), custom_call_target="tpu_custom_call" | custom-call | tf_op jit(solution)/shard_map/pallas_call | solution.py:460
  40.6 0.7 %shard_map.104 = (bf16[128,512]{1,0:T(8,128)(2,1)}, bf16[128,256]{1,0:T(8,128)(2,1)}, bf16[128,256]{1,0:T(8,128)(2,1)}) custom-call(bf16[128,512]{1,0:T(8,128)(2,1)S(1)} %get-tuple-element.6.dq, bf16[128,256]{1,0:T(8,128)(2,1)S(1)} %get-tuple-element.7.dk, bf16[128,256]{1,0:T(8,128)(2,1)S(1)} %get-tuple-element.8.dv), custom_call_target="tpu_custom_call" | custom-call | tf_op jit(solution)/shard_map/pallas_call | solution.py:481
